TPU v7x, 32 devices: a whole 2x2x4 slice. The times are simulated.
32 devices in a mesh: sub: 4 (over y, x), grp: 8 (over z, core).
Axes of the slice: x: 2, y: 2, z: 4, core: 2. Of those that a mesh axis runs over, the one named last changes fastest.
Arguments:
- applied_loads: float32 [4, 8, 64, 1536], P('sub', 'grp')
- flex_matrix: bfloat16 [4, 8, 1536, 1536], P('sub', 'grp'), as said below
- schur_matrix: bfloat16 [4, 8, 1536, 1536], P('sub', 'grp'), as said below
- corner_coupling: float32 [4, 8, 12, 1536], P('sub', 'grp'), may hold values from -0.625 to 0.625
- coarse_inverse: float32 [96, 96], replicated, as said below
- face_match: int32 [4, 8, 4, 384], P('sub', 'grp'), may hold values from 0 to 383, as said below
- corner_map: int32 [4, 8, 12], P('sub', 'grp'), may hold values from 0 to 95, as said below
Outputs:
- multipliers: float32 [4, 8, 64, 4, 384], P('sub', 'grp')
- residual: float32 [4, 8, 64, 4, 384], P('sub', 'grp')
Inputs may be any that keep to these rules, and one draw needn't show every extreme that they name: `flex_matrix`: each subdomain's matrix is symmetric positive definite. `schur_matrix`: each subdomain's matrix is symmetric positive definite. `coarse_inverse`: lower triangular with a positive diagonal. face_match[s, g, 1] is a permutation of the 384 face nodes and face_match[s+1, g, 0] is its inverse; face_match[s, g, 3] and face_match[s, g+1, 2] likewise (indices wrap). `corner_map`: the 12 entries of one subdomain are distinct; every corner unknown is named by exactly four subdomains.
All inputs are finite; a program needn't handle non-finite values.
Results may differ from a plain program's by a relative error of at most 0.0088.
Values sent between devices are 32-bit elements; how exact they have to be, the bound alone decides.
No kernel may reach another device: no remote copies, remote signals or barrier semaphores. Data moves between devices by JAX's collectives and lax.ppermute only.
A program may use at most 64 MiB of HBM per device.

v0:
```python
import functools

import jax
import jax.numpy as jnp
from jax import lax
from jax.experimental import pallas as pl
from jax.experimental.pallas import tpu as pltpu
from jax.sharding import PartitionSpec as P

HIGHEST = lax.Precision.HIGHEST
PLAIN = (((1,), (0,)), ((), ()))
LAST = (((1,), (1,)), ((), ()))
LANES = 128
SIGNS = (-1.0, 1.0, -1.0, 1.0)


def odd(axis):
    return lax.axis_index(axis) % 2 == 1


def swapped(faces, odds):
    far, near = [], []
    for (low, high), is_odd in zip((faces[0:2], faces[2:4]), odds):
        far.append(jnp.where(is_odd, high, low))
        near.append(jnp.where(is_odd, low, high))
    return far + near


def swap(face, i):
    axis = ("sub", "grp", "sub", "grp")[i]
    peers = lax.axis_size(axis)
    if i < 2:
        pairs = [(j, (j + 2 * (j % 2) - 1) % peers) for j in range(peers)]
    else:
        pairs = [(j, j ^ 1) for j in range(peers)]
    return lax.ppermute(face, axis, pairs)


def exchange(faces):
    return lax.optimization_barrier([swap(face, i) for i, face in enumerate(faces)])


def sum_over(values, axis, step, before=(), after=()):
    peers = lax.axis_size(axis)
    first = True
    while step < peers:
        count = 4 if 4 * step <= peers else 2
        others = [
            lax.ppermute(values, axis, [(i, i ^ (k * step)) for i in range(peers)])
            for k in ((2, 1, 3) if count == 4 else (1,))
        ]
        if first:
            before, others, after = lax.optimization_barrier((before, others, after))
            first = False
        if count == 4:
            values = (values + others[1]) + (others[0] + others[2])
        else:
            values = values + others[0]
        step *= count
    return values, before, after


def sum_and_exchange(faces, cases):
    far, high, near, core = faces
    size = near.shape[1]
    other = swap(core, 3)
    values = core[:cases, size:] + other[:cases, size:]
    near, values = lax.optimization_barrier((near, values))
    near = swap(near, 2)
    values, far, _ = sum_over(values, "grp", 2, [swap(far, 0)])
    far, high, values = lax.optimization_barrier((far, high, values))
    values, high, _ = sum_over(values, "sub", 1, [swap(high, 1)])
    return values, [*far, *high, near, other]


def one_hot(match_ref, i):
    row = match_ref[i : i + 1, :]
    size = row.shape[1]
    nodes = lax.broadcasted_iota(jnp.int32, (size, size), 0)
    return jnp.where(nodes == row, 1.0, 0.0).astype(jnp.bfloat16)


def parts(x, count):
    out = []
    for _ in range(count):
        part = x.astype(jnp.bfloat16)
        out.append(part)
        x = x - part.astype(jnp.float32)
    return out


def mxu(x, y, dims=PLAIN):
    return lax.dot_general(x, y, dims, preferred_element_type=jnp.float32)


def exact(x, y, dims=PLAIN):
    return lax.dot_general(x, y, dims, precision=HIGHEST, preferred_element_type=jnp.float32)


def reorder(x, hot, dims):
    rows = x.shape[0]
    both = mxu(jnp.concatenate(parts(x, 3), axis=0), hot, dims)
    return both[:rows] + both[rows : 2 * rows] + both[2 * rows :]


def turn(x, hot):
    return reorder(x, hot, LAST)


def turn_back(x, hot):
    return reorder(x, hot, PLAIN)


def jump(received, own):
    return [
        received[0] - own[0],
        own[1] - received[1],
        received[2] - own[2],
        own[3] - received[3],
    ]


def odds():
    return odd("sub"), odd("grp")


def faces_in(values):
    out = []
    for far, near, is_odd in zip(values[0:2], values[2:4], odds()):
        out += [jnp.where(is_odd, near, far), jnp.where(is_odd, far, near)]
    return out


def faces_of(ref, size):
    return [ref[:, i * size : (i + 1) * size] for i in range(4)]


def store(ref, faces):
    size = faces[0].shape[1]
    for i in range(4):
        ref[:, i * size : (i + 1) * size] = faces[i]


def store_some(ref, faces):
    size = faces[0].shape[1]
    for i, face in enumerate(faces):
        ref[:, i * size : (i + 1) * size] = face


def total(xs, ys):
    return sum(jnp.sum(x * y, axis=1, keepdims=True) for x, y in zip(xs, ys))


def blocks_of(interface):
    width = 256 if interface % 256 == 0 else interface
    return [slice(i, i + width) for i in range(0, interface, width)]


def product(matrix_ref, result_ref, left, groups):
    for block in blocks_of(matrix_ref.shape[1]):
        both = mxu(left, matrix_ref[:, block])
        at = 0
        for first, rows, count in groups:
            value = both[first : first + rows]
            for i in range(1, count):
                value = value + both[first + i * rows : first + (i + 1) * rows]
            result_ref[at : at + rows, block] = value
            at += rows


def local_order(faces, hots, count):
    split = [jnp.concatenate(parts(x, count), axis=0) for x in faces]
    split[0] = mxu(split[0], hots[0]).astype(jnp.bfloat16)
    split[2] = mxu(split[2], hots[2]).astype(jnp.bfloat16)
    return jnp.concatenate(split, axis=1)


def face_parts(faces, count):
    return jnp.concatenate(
        [jnp.concatenate(parts(x, count), axis=0) for x in faces], axis=1
    )


def turned_result(result_ref, hots):
    size = result_ref.shape[1] // 4
    own = faces_of(result_ref, size)
    own[0] = turn(own[0], hots[0])
    own[2] = turn(own[2], hots[2])
    return own


def weighted(faces):
    return [(0.5 * s) * x for s, x in zip(SIGNS, faces)]


def hots_of(hots_ref):
    size = hots_ref.shape[1]
    return [hots_ref[i * size : (i + 1) * size, :] for i in range(4)]


def signed(faces):
    return [s * x for s, x in zip(SIGNS, faces)]


def lane_is(shape, lane):
    return lax.broadcasted_iota(jnp.int32, shape, 1) == lane


def pick(values, lane):
    return jnp.sum(jnp.where(lane_is(values.shape, lane), values, 0.0), axis=1, keepdims=True)


def numbering(extra, slots, width):
    numbers = extra[slots : slots + 1, :LANES]
    nodes = lax.broadcasted_iota(jnp.int32, (width, LANES), 0).astype(jnp.float32)
    hot = jnp.where(nodes == numbers, 1.0, 0.0)
    return hot[:, : 3 * extra.shape[0]].astype(jnp.bfloat16)


def spread(extra, slots, width):
    return mxu(numbering(extra, slots, width), jnp.concatenate(parts(extra, 3), axis=0))


def partial_sums(left, coupling, extra, slots, scalars, coarse_size, width):
    out = reorder(mxu(left, coupling, LAST), numbering(extra, slots, width), LAST)
    rows = out.shape[0] // 2
    out = out[:rows] + out[rows:]
    for i, value in enumerate(scalars):
        out = out + jnp.where(lane_is(out.shape, coarse_size + i), value, 0.0)
    return out


def by_parts(x, matrix, dims):
    rows = x.shape[0]
    both = mxu(jnp.concatenate(parts(x, 3), axis=0), matrix, dims)
    both = both[:rows] + (both[rows : 2 * rows] + both[2 * rows :])
    width = both.shape[1] // 3
    return both[:, :width] + (both[:, width : 2 * width] + both[:, 2 * width :])


def coarse_solve(right, down_ref, up_ref):
    lowered = by_parts(right, down_ref[...], LAST)
    return by_parts(lowered, up_ref[...], PLAIN), jnp.sum(lowered * lowered, axis=1, keepdims=True)


def coarse_part(sums, coarse_size):
    lanes = lax.broadcasted_iota(jnp.int32, sums.shape, 1)
    return jnp.where(lanes < coarse_size, sums, 0.0)


def two_high(x):
    return jnp.concatenate(parts(x, 2), axis=0)


def two_wide(x):
    high, low = parts(x, 2)
    return jnp.concatenate(
        [jnp.concatenate([high, high], axis=1), jnp.concatenate([low, low], axis=1)], axis=0
    )


def coarse_times(coarse, *image_refs):
    rows = coarse.shape[0]
    left = two_wide(coarse)
    both = [mxu(left, image[...]) for image in image_refs]
    return jnp.concatenate([x[:rows] + x[rows:] for x in both], axis=1)


def prepare_kernel(loads_ref, match_ref, schur_ref,
                   loads_out, hots_out, schur_out, match_held, sems):
    copies = [
        pltpu.make_async_copy(x, y, sems.at[i])
        for i, (x, y) in enumerate(
            ((match_ref, match_held), (loads_ref, loads_out), (schur_ref, schur_out))
        )
    ]
    for copy in copies:
        copy.start()
    size = loads_ref.shape[1] // 4
    copies[0].wait()
    for i in range(4):
        hots_out[i * size : (i + 1) * size, :] = one_hot(match_held, i)
    copies[1].wait()
    for i in (0, 2):
        block = slice(i * size, (i + 1) * size)
        loads_out[:, block] = turn(loads_out[:, block], hots_out[block, :])
    copies[2].wait()


def extra_kernel(coupling_ref, corners_ref, inverse_ref, hots_ref,
                 extra_out, spread_out, coupling_out, down_out, up_out):
    size = hots_ref.shape[1]
    slots = coupling_ref.shape[0]
    rows = extra_out.shape[0]
    hots = hots_of(hots_ref)
    extra_out[...] = jnp.full(extra_out.shape, -1.0, jnp.float32)
    corners = corners_ref[...].astype(jnp.float32)
    for i in range(4):
        extra_out[:slots, i * size : (i + 1) * size] = coupling_ref[:, i * size : (i + 1) * size]
        for k in range(3):
            at = i * size + k * rows
            extra_out[slots : slots + 1, at : at + slots] = corners
    for i in (0, 2):
        block = slice(i * size, (i + 1) * size)
        extra_out[:slots, block] = turn(coupling_ref[:, block], hots[i])
    coupling_out[...] = jnp.concatenate(parts(extra_out[...], 3), axis=0)
    spread_out[...] = spread(extra_out[...], slots, spread_out.shape[0])
    inverse = parts(inverse_ref[...], 3)
    down_out[...] = jnp.concatenate(inverse, axis=0)
    up_out[...] = jnp.concatenate(inverse, axis=1)


def turn_matrix_kernel(matrix_ref, hots_ref, out_ref):
    size = hots_ref.shape[1]
    hots = hots_of(hots_ref)
    for i in range(4):
        rows = slice(i * size, (i + 1) * size)
        block = faces_of(matrix_ref.at[rows, :], size)
        for j in (0, 2):
            block[j] = mxu(block[j], hots[j], LAST).astype(jnp.bfloat16)
        for j in range(4):
            if i in (0, 2):
                block[j] = mxu(hots[i], block[j]).astype(jnp.bfloat16)
            out_ref[rows, j * size : (j + 1) * size] = block[j]


def first_kernel(near0, near1, near2, near3, loads_ref, hots_ref, schur_ref,
                 residual_ref, send0, send1, send2, send3, result_ref):
    cases = loads_ref.shape[0]
    size = loads_ref.shape[1] // 4
    hots = hots_of(hots_ref)
    near = faces_in([x[...] for x in (near0, near1, near2, near3)])
    for i in (1, 3):
        near[i] = reorder(near[i], hots[i], PLAIN)
    residual = jump(near, faces_of(loads_ref, size))
    store(residual_ref, residual)
    product(schur_ref, result_ref, local_order(weighted(residual), hots, 1), [(0, cases, 1)])
    for ref, value in zip(
        (send0, send1, send2, send3), swapped(turned_result(result_ref, hots), odds())
    ):
        ref[...] = value


def coarse_kernel(cases, spread_ref, far_ref, near_ref, core_ref, image_ref, rest_ref):
    width, interface = spread_ref.shape
    size = interface // 4
    slots = near_ref.shape[0] - cases - 4
    own = faces_of(spread_ref, size)
    far, near, core = [
        spread(x[cases:, :size], slots, width) for x in (far_ref, near_ref, core_ref)
    ]
    zero = jnp.zeros_like(core)
    image = jump(faces_in([far, zero, near, core]), own)
    store_some(image_ref, [two_high(x) for x in image[:2]])
    store_some(rest_ref, image[2:])


def coarse_rest_kernel(cases, rest_ref, high_ref, image_ref):
    size = rest_ref.shape[1] // 2
    width = rest_ref.shape[0]
    slots = high_ref.shape[0] - cases - 4
    share = spread(high_ref[cases:, :size], slots, width)
    zero = jnp.zeros_like(share)
    low, high = faces_in([zero, share, zero, zero])[2:]
    store_some(image_ref, [two_high(rest_ref[:, :size] + low), two_high(rest_ref[:, size:] - high)])


def direction_kernel(coarse_size, count, *refs):
    own = refs[0:4]
    near = [refs[i] for i in (4, 6, 5, 7)]
    extra_ref, coupling_ref, residual_ref, flex_ref = refs[8:12]
    n = 12
    if count > 1:
        before_ref = refs[12]
        before_free = refs[13:17]
        n = 17
    precond_ref, free0, free1, free2, free3, result_ref = refs[n:]
    size = own[0].shape[1]
    cases = residual_ref.shape[0]
    slots = extra_ref.shape[0] - 4
    precond = jump(faces_in([x[...] for x in near]), faces_in([x[...] for x in own]))
    precond = [0.5 * x for x in precond]
    store(precond_ref, precond)
    forces = signed(precond)
    left = face_parts(forces, 2)
    product(flex_ref, result_ref, left[: count * cases], [(0, cases, count)])
    free = faces_of(result_ref, size)
    extra = faces_of(extra_ref, size)
    for ref, value, rows in zip(
        (free0, free1, free2, free3), swapped(free, odds()), swapped(extra, odds())
    ):
        ref[:cases, :size] = value
        if count == 1:
            ref[cases:, :size] = rows
    scalars = [0.5 * total(faces_of(residual_ref, size), precond), total(forces, free)]
    if count > 1:
        before = signed(faces_of(before_ref, size))
        scalars.append(total(forces, faces_in([x[:cases, :size] for x in before_free])) + total(before, free))
    width = free3.shape[1] - size
    free3[:cases, size:] = partial_sums(
        left, coupling_ref[...], extra[0], slots, scalars, coarse_size, width
    )
    if count == 1:
        free3[cases:, size:] = jnp.zeros((free3.shape[0] - cases, width), jnp.float32)


def step_kernel(coarse_size, sums_ref, down_ref, up_ref, image_ref, rest_ref, own0, own1, own2, own3,
                near0, near1, near2, near3, residual_ref, hots_ref, schur_ref,
                new_ref, jump_ref, step_ref, send0, send1, send2, send3, result_ref):
    size = own0.shape[1]
    cases = sums_ref.shape[0]
    hots = hots_of(hots_ref)
    moved = jump(
        faces_in([x[:cases, :size] for x in (near0, near1, near2, near3)]),
        faces_in([x[:cases, :size] for x in (own0, own1, own2, own3)]),
    )
    store(jump_ref, moved)
    sums = sums_ref[...]
    coarse, energy = coarse_solve(coarse_part(sums, coarse_size), down_ref, up_ref)
    step = pick(sums, coarse_size) / (pick(sums, coarse_size + 1) + energy)
    step_ref[...] = jnp.broadcast_to(step, step_ref.shape)
    image = coarse_times(coarse, image_ref, rest_ref)
    residual = [
        residual_ref[:, i * size : (i + 1) * size]
        - step * (moved[i] + image[:, i * size : (i + 1) * size])
        for i in range(4)
    ]
    store(new_ref, residual)
    product(schur_ref, result_ref, local_order(weighted(residual), hots, 1), [(0, cases, 1)])
    for ref, value in zip(
        (send0, send1, send2, send3), swapped(turned_result(result_ref, hots), odds())
    ):
        ref[...] = value


def home_kernel(residual_ref, before_ref, precond_ref, jump_ref, image_ref, rest_ref, hots_ref,
                own_far, own_near, far, near,
                residual_out, before_out, precond_out, jump_out, image_out, next_out):
    size = hots_ref.shape[1]
    hots = hots_of(hots_ref)
    fields = [faces_of(x, size) for x in (residual_ref, before_ref, precond_ref, jump_ref)]
    image = [
        ref[:, block] for ref in (image_ref, rest_ref) for block in (slice(size), slice(size, None))
    ]
    for i in (0, 2):
        image[i] = mxu(image[i], hots[i]).astype(jnp.bfloat16)
        for field in fields:
            field[i] = turn_back(field[i], hots[i])
    low, high = faces_in([far[...], far[...], near[...], near[...]])[:2]
    own = [own_far[...], own_near[...]]
    own_low, own_high = faces_in([own[0], own[0], own[1], own[1]])[:2]
    store_some(next_out, [turn_back(low - own_low, hots[0]), own_high - high])
    store(image_out, image)
    for ref, field in zip((residual_out, before_out, precond_out, jump_out), fields):
        store(ref, field)


def last_kernel(coarse_size, first_ref, sums_ref, down_ref, up_ref, step_ref, residual_ref, before_ref,
                precond_ref, jump_ref, image_ref, next_ref, hots_ref, own_high, own_core,
                high_ref, core_ref, multipliers_ref, out_ref):
    size = hots_ref.shape[1]
    hots = hots_of(hots_ref)
    grp = [high_ref[...], core_ref[:, :size]]
    own = [own_high[...], own_core[:, :size]]
    low, high = faces_in([grp[0], grp[0], grp[1], grp[1]])[2:]
    own_low, own_high = faces_in([own[0], own[0], own[1], own[1]])[2:]
    following = [
        next_ref[:, :size],
        next_ref[:, size:],
        turn_back(low - own_low, hots[2]),
        own_high - high,
    ]
    first = first_ref[...]
    sums = sums_ref[...]
    beta = pick(sums, coarse_size) / pick(first, coarse_size)
    right = coarse_part(sums, coarse_size) + beta * coarse_part(first, coarse_size)
    coarse, energy = coarse_solve(right, down_ref, up_ref)
    local = pick(sums, coarse_size + 1) + beta * (
        pick(sums, coarse_size + 2) + beta * pick(first, coarse_size + 1)
    )
    step = pick(sums, coarse_size) / (local + energy)
    step_before = step_ref[:, 0:1]
    image = coarse_times(coarse, image_ref)
    for i in range(4):
        block = slice(i * size, (i + 1) * size)
        moved = following[i] + beta * jump_ref[:, block] + image[:, block]
        out_ref[:, i, :] = residual_ref[:, block] - step * moved
        before = before_ref[:, block]
        direction = precond_ref[:, block] + beta * before
        multipliers_ref[:, i, :] = step_before * before + step * direction


VMEM = pl.BlockSpec(memory_space=pltpu.VMEM)
OUTSIDE = pl.BlockSpec(memory_space=pltpu.HBM)


def call(kernel, args, outs, scratch=(), outside=(), flops=0):
    specs = [OUTSIDE if i in outside else VMEM for i in range(len(args))]
    shapes = [(x, jnp.float32) if isinstance(x[0], int) else x for x in outs]
    return pl.pallas_call(
        kernel,
        in_specs=specs,
        out_specs=[VMEM] * len(outs),
        out_shape=[jax.ShapeDtypeStruct(*x) for x in shapes],
        scratch_shapes=list(scratch),
        compiler_params=pltpu.CompilerParams(vmem_limit_bytes=28 * 2**20),
        cost_estimate=pl.CostEstimate(flops=flops, bytes_accessed=2**22, transcendentals=0),
    )(*args)


def shards(
    applied_loads,
    flex_matrix,
    schur_matrix,
    corner_coupling,
    coarse_inverse,
    face_match,
    corner_map,
):
    loads = applied_loads[0, 0]
    flex = flex_matrix[0, 0]
    schur = schur_matrix[0, 0]
    match = face_match[0, 0]
    cases, interface = loads.shape
    size = interface // 4
    slots = corner_coupling.shape[2]
    coarse_size = coarse_inverse.shape[0]
    width = -(-(coarse_size + 3) // LANES) * LANES
    work = 2 * cases * interface * interface

    inverse = jnp.pad(coarse_inverse, ((0, width - coarse_size), (0, width - coarse_size)))
    field = (cases, interface)
    face = (cases, size)
    result = pltpu.VMEM(field, jnp.float32)
    both_parts = ((2 * width, interface), jnp.bfloat16)

    held = [pltpu.with_memory_space_constraint(x, pltpu.HBM) for x in (loads, match, schur)]
    sends = swapped(
        [loads[:, i * size : (i + 1) * size] for i in range(4)], (odd("sub"), odd("grp"))
    )
    sends = lax.optimization_barrier(sends)
    near = exchange(sends)
    loads, hots, schur = call(
        prepare_kernel,
        held,
        [field, ((4 * size, size), jnp.bfloat16), (schur.shape, jnp.bfloat16)],
        [pltpu.VMEM(match.shape, jnp.int32), pltpu.SemaphoreType.DMA((3,))],
        outside=(0, 1, 2),
        flops=work,
    )
    residual, *own_first = call(
        first_kernel, [*near, loads, hots, schur], [field] + [face] * 4, [result], flops=work
    )
    near = exchange(own_first)
    residual, coupling, corners, flex = lax.optimization_barrier(
        (residual, corner_coupling[0, 0], corner_map[0], flex)
    )
    (flex,) = call(
        turn_matrix_kernel, [flex, hots], [(flex.shape, jnp.bfloat16)], flops=2 * work
    )
    extra, own_spread, coupling, down, up = call(
        extra_kernel,
        [coupling, corners, inverse, hots],
        [
            (slots + 4, interface),
            (width, interface),
            ((3 * (slots + 4), interface), jnp.bfloat16),
            ((3 * width, width), jnp.bfloat16),
            ((width, 3 * width), jnp.bfloat16),
        ],
        flops=work // 4,
    )
    before, *own_free = call(
        functools.partial(direction_kernel, coarse_size, 1),
        [*own_first, near[0], near[2], near[1], near[3], extra, coupling, residual, flex],
        [field] + [(cases + slots + 4, size)] * 3 + [(cases + slots + 4, size + width)],
        [result],
        flops=work,
    )
    first_sums, near = sum_and_exchange(own_free, cases)
    half = ((2 * width, interface // 2), jnp.bfloat16)
    image, rest = call(
        functools.partial(coarse_kernel, cases),
        [own_spread, near[0], near[2], near[3]],
        [half, (width, interface // 2)],
        flops=work // 4,
    )
    (rest,) = call(
        functools.partial(coarse_rest_kernel, cases), [rest, near[1]], [half], flops=work // 8
    )
    residual, moved, step, *own = call(
        functools.partial(step_kernel, coarse_size),
        [first_sums, down, up, image, rest, *own_free, *near, residual, hots, schur],
        [field, field, (cases, LANES)] + [face] * 4,
        [result],
        flops=work,
    )
    near = exchange(own)
    precond, *own = call(
        functools.partial(direction_kernel, coarse_size, 2),
        [*own, near[0], near[2], near[1], near[3], extra, coupling, residual, flex, before, *own_free],
        [field] + [face] * 3 + [(cases, size + width)],
        [result],
        flops=work,
    )
    sums, near = sum_and_exchange(own, cases)
    fields = call(
        home_kernel,
        [residual, before, precond, moved, image, rest, hots, own[0], own[2], near[0], near[2]],
        [field] * 4 + [both_parts, (cases, 2 * size)],
        flops=work // 2,
    )
    layout = (cases, 4, size)
    multipliers, residual = call(
        functools.partial(last_kernel, coarse_size),
        [first_sums, sums, down, up, step, *fields, hots, own[1], own[3], near[1], near[3]],
        [layout, layout],
        flops=work // 4,
    )
    return multipliers[None, None], residual[None, None]


def solution(mesh):
    return jax.shard_map(
        shards,
        mesh=mesh,
        in_specs=(
            P("sub", "grp", None, None),
            P("sub", "grp", None, None),
            P("sub", "grp", None, None),
            P("sub", "grp", None, None),
            P(),
            P("sub", "grp", None, None),
            P("sub", "grp", None),
        ),
        out_specs=(P("sub", "grp", None, None, None), P("sub", "grp", None, None, None)),
        check_vma=False,
    )
```

profile of v0, /device:TPU:0, one launch (start us, length us, event | category | flops | bytes accessed | tf_op | source)
XLA Modules:
  0.0 67.4 jit_solution(15901986116069479978)
XLA Ops:
  0.6 1.1 %slice_select_fusion = (f32[64,384]{1,0:T(8,128)S(1)}, f32[64,384]{1,0:T(8,128)S(1)}, f32[64,384]{1,0:T(8,128)S(1)}, f32[64,384]{1,0:T(8,128)S(1)}) fusion(f32[64,1536]{1,0:T(8,128)} %bitcast.16, pred[]{:T(512)S(6)} %eq.10, pred[]{:T(512)S(6)} %eq.9), kind=kLoop, calls=%fused_computation.1 | loop fusion | flops 98304 | bytes 786434 | tf_op jit(solution)/shard_map/jit(_where)/select_n | solution.py:25
  1.7 4.0 %collective-permute-start = (f32[64,384]{1,0:T(8,128)S(1)}, f32[64,384]{1,0:T(8,128)S(1)}, u32[]{:S(2)}, u32[]{:S(2)}) collective-permute-start(f32[64,384]{1,0:T(8,128)S(1)} %get-tuple-element.88), channel_id=1, source_target_pairs={{0,24},{8,16},{16,8},{24,0},{1,25},{9,17},{17,9},{25,1},{2,26},{10... | collective-permute-start | bytes 294920 | tf_op jit(solution)/shard_map/ppermute | solution.py:36
  5.7 2.8 %collective-permute-start.1 = (f32[64,384]{1,0:T(8,128)S(1)}, f32[64,384]{1,0:T(8,128)S(1)}, u32[]{:S(2)}, u32[]{:S(2)}) collective-permute-start(f32[64,384]{1,0:T(8,128)S(1)} %get-tuple-element.89), channel_id=1, source_target_pairs={{0,7},{1,2},{2,1},{3,4},{4,3},{5,6},{6,5},{7,0},{8,15},{9,10},{10,... | collective-permute-start | bytes 294920 | tf_op jit(solution)/shard_map/ppermute | solution.py:36
  9.0 2.7 %shard_map.86 = (f32[64,1536]{1,0:T(8,128)S(1)}, bf16[1536,384]{1,0:T(8,128)(2,1)S(1)}, bf16[1536,1536]{1,0:T(8,128)(2,1)S(1)}) custom-call(f32[64,1536]{1,0:T(8,128)} %bitcast.17, s32[4,384]{1,0:T(4,128)} %bitcast.18, bf16[1536,1536]{1,0:T(8,128)(2,1)} %bitcast.15), custom_call_target="tpu_custom_call" | custom-call | flops 301989888 | bytes 4194304 | tf_op jit(solution)/shard_map/pallas_call | solution.py:500
  13.1 1.5 %shard_map.87 = (f32[64,1536]{1,0:T(8,128)S(1)}, f32[64,384]{1,0:T(8,128)S(1)}, f32[64,384]{1,0:T(8,128)S(1)}, f32[64,384]{1,0:T(8,128)S(1)}, f32[64,384]{1,0:T(8,128)S(1)}) custom-call(f32[64,384]{1,0:T(8,128)S(1)} %collective-permute-done.near0, f32[64,384]{1,0:T(8,128)S(1)} %collective-permute-done.1.near1, f32[64,384]{1,0:T(8,128)S(1)} %collective-permute-done.2.near2, ...), custom_call_target="tpu_custom_call" | custom-call | flops 301989888 | bytes 4194304 | tf_op jit(solution)/shard_map/pallas_call | solution.py:500
  15.1 1.0 %collective-permute-start.5 = (f32[64,384]{1,0:T(8,128)S(1)}, f32[64,384]{1,0:T(8,128)S(1)}, u32[]{:S(2)}, u32[]{:S(2)}) collective-permute-start(f32[64,384]{1,0:T(8,128)S(1)} %get-tuple-element.100.refs_1_), channel_id=1, source_target_pairs={{0,7},{1,2},{2,1},{3,4},{4,3},{5,6},{6,5},{7,0},{8,15},{9,10},{10,... | collective-permute-start | bytes 294920 | tf_op jit(solution)/shard_map/ppermute | solution.py:36
  16.1 1.5 %collective-permute-start.6 = (f32[64,384]{1,0:T(8,128)S(1)}, f32[64,384]{1,0:T(8,128)S(1)}, u32[]{:S(2)}, u32[]{:S(2)}) collective-permute-start(f32[64,384]{1,0:T(8,128)S(1)} %get-tuple-element.101.refs_2_), channel_id=1, source_target_pairs={{0,8},{8,0},{16,24},{24,16},{1,9},{9,1},{17,25},{25,17},{2,10},{10... | collective-permute-start | bytes 294920 | tf_op jit(solution)/shard_map/ppermute | solution.py:36
  18.2 3.2 %shard_map.89.refs_11_ = bf16[1536,1536]{1,0:T(8,128)(2,1)S(1)} custom-call(bf16[1536,1536]{1,0:T(8,128)(2,1)S(1)} %bitcast.12, bf16[1536,384]{1,0:T(8,128)(2,1)S(1)} %get-tuple-element.97.hots_ref), custom_call_target="tpu_custom_call" | custom-call | flops 603979776 | bytes 4194304 | tf_op jit(solution)/shard_map/pallas_call | solution.py:500
  21.4 1.2 %shard_map.90 = (f32[64,1536]{1,0:T(8,128)S(1)}, f32[80,384]{1,0:T(8,128)S(1)}, f32[80,384]{1,0:T(8,128)S(1)}, f32[80,384]{1,0:T(8,128)S(1)}, f32[80,512]{1,0:T(8,128)S(1)}) custom-call(f32[64,384]{1,0:T(8,128)S(1)} %get-tuple-element.99.refs_0_, f32[64,384]{1,0:T(8,128)S(1)} %get-tuple-element.100.refs_1_, f32[64,384]{1,0:T(8,128)S(1)} %get-tuple-element.101.refs_2_, ...), custom_call_target="tpu_custom_call" | custom-call | flops 301989888 | bytes 4194304 | tf_op jit(solution)/shard_map/pallas_call | solution.py:500
  23.2 1.6 %collective-permute-start.8 = (f32[80,384]{1,0:T(8,128)S(1)}, f32[80,384]{1,0:T(8,128)S(1)}, u32[]{:S(2)}, u32[]{:S(2)}) collective-permute-start(f32[80,384]{1,0:T(8,128)S(1)} %get-tuple-element.114.own0.refs_13_), channel_id=1, source_target_pairs={{0,24},{8,16},{16,8},{24,0},{1,25},{9,17},{17,9},{25,1},{2,26},{10... | collective-permute-start | bytes 368648 | tf_op jit(solution)/shard_map/ppermute | solution.py:36
  24.8 2.2 %collective-permute-start.12 = (f32[64,128]{1,0:T(8,128)S(1)}, f32[64,128]{1,0:T(8,128)S(1)}, u32[]{:S(2)}, u32[]{:S(2)}) collective-permute-start(f32[64,128]{1,0:T(8,128)S(1)} %slice_add_fusion.1), channel_id=1, source_target_pairs={{0,6},{1,7},{2,4},{3,5},{4,2},{5,3},{6,0},{7,1},{8,14},{9,15},{10,... | collective-permute-start | bytes 98312 | tf_op jit(solution)/shard_map/ppermute | solution.py:49
  27.0 2.2 %collective-permute-start.10 = (f32[64,128]{1,0:T(8,128)S(1)}, f32[64,128]{1,0:T(8,128)S(1)}, u32[]{:S(2)}, u32[]{:S(2)}) collective-permute-start(f32[64,128]{1,0:T(8,128)S(1)} %slice_add_fusion.1), channel_id=1, source_target_pairs={{0,4},{1,5},{2,6},{3,7},{4,0},{5,1},{6,2},{7,3},{8,12},{9,13},{10,... | collective-permute-start | bytes 98312 | tf_op jit(solution)/shard_map/ppermute | solution.py:49
  29.3 1.4 %collective-permute-start.17 = (f32[80,384]{1,0:T(8,128)S(1)}, f32[80,384]{1,0:T(8,128)S(1)}, u32[]{:S(2)}, u32[]{:S(2)}) collective-permute-start(f32[80,384]{1,0:T(8,128)S(1)} %get-tuple-element.132.own2.refs_15_), channel_id=1, source_target_pairs={{0,8},{8,0},{16,24},{24,16},{1,9},{9,1},{17,25},{25,17},{2,10},{10... | collective-permute-start | bytes 368648 | tf_op jit(solution)/shard_map/ppermute | solution.py:36
  31.3 0.9 %collective-permute-done.10 = f32[64,128]{1,0:T(8,128)S(1)} collective-permute-done((f32[64,128]{1,0:T(8,128)S(1)}, f32[64,128]{1,0:T(8,128)S(1)}, u32[]{:S(2)}, u32[]{:S(2)}) %collective-permute-start.10) | collective-permute-done | bytes 32800 | tf_op jit(solution)/shard_map/ppermute | solution.py:49
  32.3 1.5 %collective-permute-start.16 = (f32[64,128]{1,0:T(8,128)S(1)}, f32[64,128]{1,0:T(8,128)S(1)}, u32[]{:S(2)}, u32[]{:S(2)}) collective-permute-start(f32[64,128]{1,0:T(8,128)S(1)} %add_add_fusion.3), channel_id=1, source_target_pairs={{0,24},{8,16},{16,8},{24,0},{1,25},{9,17},{17,9},{25,1},{2,26},{10... | collective-permute-start | bytes 98312 | tf_op jit(solution)/shard_map/ppermute | solution.py:49
  33.8 1.4 %collective-permute-start.15 = (f32[64,128]{1,0:T(8,128)S(1)}, f32[64,128]{1,0:T(8,128)S(1)}, u32[]{:S(2)}, u32[]{:S(2)}) collective-permute-start(f32[64,128]{1,0:T(8,128)S(1)} %add_add_fusion.3), channel_id=1, source_target_pairs={{0,8},{8,0},{16,24},{24,16},{1,9},{9,1},{17,25},{25,17},{2,10},{10... | collective-permute-start | bytes 98312 | tf_op jit(solution)/shard_map/ppermute | solution.py:49
  36.1 1.0 %collective-permute-done.16 = f32[64,128]{1,0:T(8,128)S(1)} collective-permute-done((f32[64,128]{1,0:T(8,128)S(1)}, f32[64,128]{1,0:T(8,128)S(1)}, u32[]{:S(2)}, u32[]{:S(2)}) %collective-permute-start.16) | collective-permute-done | bytes 32800 | tf_op jit(solution)/shard_map/ppermute | solution.py:49
  37.9 1.3 %collective-permute-done.14 = f32[64,128]{1,0:T(8,128)S(1)} collective-permute-done((f32[64,128]{1,0:T(8,128)S(1)}, f32[64,128]{1,0:T(8,128)S(1)}, u32[]{:S(2)}, u32[]{:S(2)}) %collective-permute-start.14) | collective-permute-done | bytes 32800 | tf_op jit(solution)/shard_map/ppermute | solution.py:49
  39.5 1.9 %shard_map.93 = (f32[64,1536]{1,0:T(8,128)S(1)}, f32[64,1536]{1,0:T(8,128)S(1)}, f32[64,128]{1,0:T(8,128)S(1)}, f32[64,384]{1,0:T(8,128)S(1)}, f32[64,384]{1,0:T...) custom-call(f32[64,128]{1,0:T(8,128)S(1)} %add_add_fusion.2.sums_ref.first_ref, ...), custom_call_target="tpu_custom_call" | custom-call | flops 301989888 | bytes 4194304 | tf_op jit(solution)/shard_map/pallas_call | solution.py:500
  41.4 1.7 %collective-permute-start.18 = (f32[64,384]{1,0:T(8,128)S(1)}, f32[64,384]{1,0:T(8,128)S(1)}, u32[]{:S(2)}, u32[]{:S(2)}) collective-permute-start(f32[64,384]{1,0:T(8,128)S(1)} %get-tuple-element.136.refs_0_), channel_id=1, source_target_pairs={{0,24},{8,16},{16,8},{24,0},{1,25},{9,17},{17,9},{25,1},{2,26},{10... | collective-permute-start | bytes 294920 | tf_op jit(solution)/shard_map/ppermute | solution.py:36
  43.0 1.3 %collective-permute-start.19 = (f32[64,384]{1,0:T(8,128)S(1)}, f32[64,384]{1,0:T(8,128)S(1)}, u32[]{:S(2)}, u32[]{:S(2)}) collective-permute-start(f32[64,384]{1,0:T(8,128)S(1)} %get-tuple-element.137.refs_1_), channel_id=1, source_target_pairs={{0,7},{1,2},{2,1},{3,4},{4,3},{5,6},{6,5},{7,0},{8,15},{9,10},{10,... | collective-permute-start | bytes 294920 | tf_op jit(solution)/shard_map/ppermute | solution.py:36
  44.9 2.2 %collective-permute-done.18.refs_4_ = f32[64,384]{1,0:T(8,128)S(1)} collective-permute-done((f32[64,384]{1,0:T(8,128)S(1)}, f32[64,384]{1,0:T(8,128)S(1)}, u32[]{:S(2)}, u32[]{:S(2)}) %collective-permute-start.18) | collective-permute-done | bytes 98336 | tf_op jit(solution)/shard_map/ppermute | solution.py:36
  47.1 1.7 %collective-permute-done.19.refs_6_ = f32[64,384]{1,0:T(8,128)S(1)} collective-permute-done((f32[64,384]{1,0:T(8,128)S(1)}, f32[64,384]{1,0:T(8,128)S(1)}, u32[]{:S(2)}, u32[]{:S(2)}) %collective-permute-start.19) | collective-permute-done | bytes 98336 | tf_op jit(solution)/shard_map/ppermute | solution.py:36
  49.4 1.2 %shard_map.94 = (f32[64,1536]{1,0:T(8,128)S(1)}, f32[64,384]{1,0:T(8,128)S(1)}, f32[64,384]{1,0:T(8,128)S(1)}, f32[64,384]{1,0:T(8,128)S(1)}, f32[64,512]{1,0:T(8,128)S(1)}) custom-call(f32[64,384]{1,0:T(8,128)S(1)} %get-tuple-element.136.refs_0_, f32[64,384]{1,0:T(8,128)S(1)} %get-tuple-element.137.refs_1_, f32[64,384]{1,0:T(8,128)S(1)} %get-tuple-element.138.refs_2_, ...), custom_call_target="tpu_custom_call" | custom-call | flops 301989888 | bytes 4194304 | tf_op jit(solution)/shard_map/pallas_call | solution.py:500
  50.6 1.4 %collective-permute-start.22 = (f32[64,384]{1,0:T(8,128)S(1)}, f32[64,384]{1,0:T(8,128)S(1)}, u32[]{:S(2)}, u32[]{:S(2)}) collective-permute-start(f32[64,384]{1,0:T(8,128)S(1)} %get-tuple-element.146.own_far), channel_id=1, source_target_pairs={{0,24},{8,16},{16,8},{24,0},{1,25},{9,17},{17,9},{25,1},{2,26},{10... | collective-permute-start | bytes 294920 | tf_op jit(solution)/shard_map/ppermute | solution.py:36
  52.0 1.9 %collective-permute-start.26 = (f32[64,128]{1,0:T(8,128)S(1)}, f32[64,128]{1,0:T(8,128)S(1)}, u32[]{:S(2)}, u32[]{:S(2)}) collective-permute-start(f32[64,128]{1,0:T(8,128)S(1)} %slice_add_fusion), channel_id=1, source_target_pairs={{0,6},{1,7},{2,4},{3,5},{4,2},{5,3},{6,0},{7,1},{8,14},{9,15},{10,... | collective-permute-start | bytes 98312 | tf_op jit(solution)/shard_map/ppermute | solution.py:49
  53.9 2.6 %collective-permute-start.24 = (f32[64,128]{1,0:T(8,128)S(1)}, f32[64,128]{1,0:T(8,128)S(1)}, u32[]{:S(2)}, u32[]{:S(2)}) collective-permute-start(f32[64,128]{1,0:T(8,128)S(1)} %slice_add_fusion), channel_id=1, source_target_pairs={{0,4},{1,5},{2,6},{3,7},{4,0},{5,1},{6,2},{7,3},{8,12},{9,13},{10,... | collective-permute-start | bytes 98312 | tf_op jit(solution)/shard_map/ppermute | solution.py:49
  59.5 1.6 %collective-permute-start.30 = (f32[64,128]{1,0:T(8,128)S(1)}, f32[64,128]{1,0:T(8,128)S(1)}, u32[]{:S(2)}, u32[]{:S(2)}) collective-permute-start(f32[64,128]{1,0:T(8,128)S(1)} %add_add_fusion.1), channel_id=1, source_target_pairs={{0,24},{8,16},{16,8},{24,0},{1,25},{9,17},{17,9},{25,1},{2,26},{10... | collective-permute-start | bytes 98312 | tf_op jit(solution)/shard_map/ppermute | solution.py:49
  61.6 1.3 %collective-permute-start.28 = (f32[64,128]{1,0:T(8,128)S(1)}, f32[64,128]{1,0:T(8,128)S(1)}, u32[]{:S(2)}, u32[]{:S(2)}) collective-permute-start(f32[64,128]{1,0:T(8,128)S(1)} %add_add_fusion.1), channel_id=1, source_target_pairs={{0,16},{8,24},{16,0},{24,8},{1,17},{9,25},{17,1},{25,9},{2,18},{10... | collective-permute-start | bytes 98312 | tf_op jit(solution)/shard_map/ppermute | solution.py:49
  63.0 1.3 %shard_map.95 = (f32[64,1536]{1,0:T(8,128)S(1)}, f32[64,1536]{1,0:T(8,128)S(1)}, f32[64,1536]{1,0:T(8,128)S(1)}, f32[64,1536]{1,0:T(8,128)S(1)}, bf16[256,1536]{1,0:T(8,128)(2,1)S(1)}, /*index=5*/f32[64,768]{1,0:T(8,128)S(1)}) custom-call(f32[64,1536]{1,0:T(8,128)S(1)} %get-tuple-element.144.refs_10_.residual_ref, ...), custom_call_target="tpu_custom_call" | custom-call | flops 150994944 | bytes 4194304 | tf_op jit(solution)/shard_map/pallas_call | solution.py:500
  64.3 0.9 %collective-permute-done.29 = f32[64,128]{1,0:T(8,128)S(1)} collective-permute-done((f32[64,128]{1,0:T(8,128)S(1)}, f32[64,128]{1,0:T(8,128)S(1)}, u32[]{:S(2)}, u32[]{:S(2)}) %collective-permute-start.29) | collective-permute-done | bytes 32800 | tf_op jit(solution)/shard_map/ppermute | solution.py:49
  65.8 1.6 %shard_map.96 = (f32[64,4,384]{2,1,0:T(4,128)}, f32[64,4,384]{2,1,0:T(4,128)}) custom-call(f32[64,128]{1,0:T(8,128)S(1)} %add_add_fusion.2.sums_ref.first_ref, f32[64,128]{1,0:T(8,128)S(1)} %add_add_fusion.sums_ref, bf16[384,128]{1,0:T(8,128)(2,1)S(1)} %get-tuple-element.128.down_ref, bf16[128,384]{1,0:T(8,128)(2,1)S(1)} %get-tuple-element.129.up_ref, ...), custom_call_target="tpu_custom_call" | custom-call | flops 75497472 | bytes 4194304 | tf_op jit(solution)/shard_map/pallas_call | solution.py:500
  (63 shorter events, 11.7 us)
Async XLA Ops:
  1.7 9.9 %collective-permute-start = (f32[64,384]{1,0:T(8,128)S(1)}, f32[64,384]{1,0:T(8,128)S(1)}, u32[]{:S(2)}, u32[]{:S(2)}) collective-permute-start(f32[64,384]{1,0:T(8,128)S(1)} %get-tuple-element.88), channel_id=1, source_target_pairs={{0,24},{8,16},{16,8},{24,0},{1,25},{9,17},{17,9},{25,1},{2,26},{10... | collective-permute-start | bytes 294920 | tf_op jit(solution)/shard_map/ppermute | solution.py:36
  5.7 6.6 %collective-permute-start.1 = (f32[64,384]{1,0:T(8,128)S(1)}, f32[64,384]{1,0:T(8,128)S(1)}, u32[]{:S(2)}, u32[]{:S(2)}) collective-permute-start(f32[64,384]{1,0:T(8,128)S(1)} %get-tuple-element.89), channel_id=1, source_target_pairs={{0,7},{1,2},{2,1},{3,4},{4,3},{5,6},{6,5},{7,0},{8,15},{9,10},{10,... | collective-permute-start | bytes 294920 | tf_op jit(solution)/shard_map/ppermute | solution.py:36
  8.4 4.6 %collective-permute-start.2 = (f32[64,384]{1,0:T(8,128)S(1)}, f32[64,384]{1,0:T(8,128)S(1)}, u32[]{:S(2)}, u32[]{:S(2)}) collective-permute-start(f32[64,384]{1,0:T(8,128)S(1)} %get-tuple-element.90), channel_id=1, source_target_pairs={{0,8},{8,0},{16,24},{24,16},{1,9},{9,1},{17,25},{25,17},{2,10},{10... | collective-permute-start | bytes 294920 | tf_op jit(solution)/shard_map/ppermute | solution.py:36
  9.0 4.1 %collective-permute-start.3 = (f32[64,384]{1,0:T(8,128)S(1)}, f32[64,384]{1,0:T(8,128)S(1)}, u32[]{:S(2)}, u32[]{:S(2)}) collective-permute-start(f32[64,384]{1,0:T(8,128)S(1)} %get-tuple-element.91), channel_id=1, source_target_pairs={{0,1},{1,0},{2,3},{3,2},{4,5},{5,4},{6,7},{7,6},{8,9},{9,8},{10,11... | collective-permute-start | bytes 294920 | tf_op jit(solution)/shard_map/ppermute | solution.py:36
  14.6 6.8 %collective-permute-start.4 = (f32[64,384]{1,0:T(8,128)S(1)}, f32[64,384]{1,0:T(8,128)S(1)}, u32[]{:S(2)}, u32[]{:S(2)}) collective-permute-start(f32[64,384]{1,0:T(8,128)S(1)} %get-tuple-element.99.refs_0_), channel_id=1, source_target_pairs={{0,24},{8,16},{16,8},{24,0},{1,25},{9,17},{17,9},{25,1},{2,26},{10... | collective-permute-start | bytes 294920 | tf_op jit(solution)/shard_map/ppermute | solution.py:36
  15.1 6.2 %collective-permute-start.5 = (f32[64,384]{1,0:T(8,128)S(1)}, f32[64,384]{1,0:T(8,128)S(1)}, u32[]{:S(2)}, u32[]{:S(2)}) collective-permute-start(f32[64,384]{1,0:T(8,128)S(1)} %get-tuple-element.100.refs_1_), channel_id=1, source_target_pairs={{0,7},{1,2},{2,1},{3,4},{4,3},{5,6},{6,5},{7,0},{8,15},{9,10},{10,... | collective-permute-start | bytes 294920 | tf_op jit(solution)/shard_map/ppermute | solution.py:36
  16.1 5.3 %collective-permute-start.6 = (f32[64,384]{1,0:T(8,128)S(1)}, f32[64,384]{1,0:T(8,128)S(1)}, u32[]{:S(2)}, u32[]{:S(2)}) collective-permute-start(f32[64,384]{1,0:T(8,128)S(1)} %get-tuple-element.101.refs_2_), channel_id=1, source_target_pairs={{0,8},{8,0},{16,24},{24,16},{1,9},{9,1},{17,25},{25,17},{2,10},{10... | collective-permute-start | bytes 294920 | tf_op jit(solution)/shard_map/ppermute | solution.py:36
  17.6 3.8 %collective-permute-start.7 = (f32[64,384]{1,0:T(8,128)S(1)}, f32[64,384]{1,0:T(8,128)S(1)}, u32[]{:S(2)}, u32[]{:S(2)}) collective-permute-start(f32[64,384]{1,0:T(8,128)S(1)} %get-tuple-element.102.refs_3_), channel_id=1, source_target_pairs={{0,1},{1,0},{2,3},{3,2},{4,5},{5,4},{6,7},{7,6},{8,9},{9,8},{10,11... | collective-permute-start | bytes 294920 | tf_op jit(solution)/shard_map/ppermute | solution.py:36
  22.6 2.2 %collective-permute-start.9 = (f32[80,512]{1,0:T(8,128)S(1)}, f32[80,512]{1,0:T(8,128)S(1)}, u32[]{:S(2)}, u32[]{:S(2)}) collective-permute-start(f32[80,512]{1,0:T(8,128)S(1)} %get-tuple-element.116.own3.refs_16_), channel_id=1, source_target_pairs={{0,1},{1,0},{2,3},{3,2},{4,5},{5,4},{6,7},{7,6},{8,9},{9,8},{10,11... | collective-permute-start | bytes 491528 | tf_op jit(solution)/shard_map/ppermute | solution.py:36
  23.2 7.5 %collective-permute-start.8 = (f32[80,384]{1,0:T(8,128)S(1)}, f32[80,384]{1,0:T(8,128)S(1)}, u32[]{:S(2)}, u32[]{:S(2)}) collective-permute-start(f32[80,384]{1,0:T(8,128)S(1)} %get-tuple-element.114.own0.refs_13_), channel_id=1, source_target_pairs={{0,24},{8,16},{16,8},{24,0},{1,25},{9,17},{17,9},{25,1},{2,26},{10... | collective-permute-start | bytes 368648 | tf_op jit(solution)/shard_map/ppermute | solution.py:36
  24.8 5.8 %collective-permute-start.12 = (f32[64,128]{1,0:T(8,128)S(1)}, f32[64,128]{1,0:T(8,128)S(1)}, u32[]{:S(2)}, u32[]{:S(2)}) collective-permute-start(f32[64,128]{1,0:T(8,128)S(1)} %slice_add_fusion.1), channel_id=1, source_target_pairs={{0,6},{1,7},{2,4},{3,5},{4,2},{5,3},{6,0},{7,1},{8,14},{9,15},{10,... | collective-permute-start | bytes 98312 | tf_op jit(solution)/shard_map/ppermute | solution.py:49
  27.0 4.3 %collective-permute-start.11 = (f32[64,128]{1,0:T(8,128)S(1)}, f32[64,128]{1,0:T(8,128)S(1)}, u32[]{:S(2)}, u32[]{:S(2)}) collective-permute-start(f32[64,128]{1,0:T(8,128)S(1)} %slice_add_fusion.1), channel_id=1, source_target_pairs={{0,2},{1,3},{2,0},{3,1},{4,6},{5,7},{6,4},{7,5},{8,10},{9,11},{10,... | collective-permute-start | bytes 98312 | tf_op jit(solution)/shard_map/ppermute | solution.py:49
  27.0 5.2 %collective-permute-start.10 = (f32[64,128]{1,0:T(8,128)S(1)}, f32[64,128]{1,0:T(8,128)S(1)}, u32[]{:S(2)}, u32[]{:S(2)}) collective-permute-start(f32[64,128]{1,0:T(8,128)S(1)} %slice_add_fusion.1), channel_id=1, source_target_pairs={{0,4},{1,5},{2,6},{3,7},{4,0},{5,1},{6,2},{7,3},{8,12},{9,13},{10,... | collective-permute-start | bytes 98312 | tf_op jit(solution)/shard_map/ppermute | solution.py:49
  29.3 6.6 %collective-permute-start.17 = (f32[80,384]{1,0:T(8,128)S(1)}, f32[80,384]{1,0:T(8,128)S(1)}, u32[]{:S(2)}, u32[]{:S(2)}) collective-permute-start(f32[80,384]{1,0:T(8,128)S(1)} %get-tuple-element.132.own2.refs_15_), channel_id=1, source_target_pairs={{0,8},{8,0},{16,24},{24,16},{1,9},{9,1},{17,25},{25,17},{2,10},{10... | collective-permute-start | bytes 368648 | tf_op jit(solution)/shard_map/ppermute | solution.py:36
  32.2 7.0 %collective-permute-start.13 = (f32[80,384]{1,0:T(8,128)S(1)}, f32[80,384]{1,0:T(8,128)S(1)}, u32[]{:S(2)}, u32[]{:S(2)}) collective-permute-start(f32[80,384]{1,0:T(8,128)S(1)} %get-tuple-element.124.own1.refs_14_), channel_id=1, source_target_pairs={{0,7},{1,2},{2,1},{3,4},{4,3},{5,6},{6,5},{7,0},{8,15},{9,10},{10,... | collective-permute-start | bytes 368648 | tf_op jit(solution)/shard_map/ppermute | solution.py:36
  32.3 4.9 %collective-permute-start.16 = (f32[64,128]{1,0:T(8,128)S(1)}, f32[64,128]{1,0:T(8,128)S(1)}, u32[]{:S(2)}, u32[]{:S(2)}) collective-permute-start(f32[64,128]{1,0:T(8,128)S(1)} %add_add_fusion.3), channel_id=1, source_target_pairs={{0,24},{8,16},{16,8},{24,0},{1,25},{9,17},{17,9},{25,1},{2,26},{10... | collective-permute-start | bytes 98312 | tf_op jit(solution)/shard_map/ppermute | solution.py:49
  33.8 4.2 %collective-permute-start.15 = (f32[64,128]{1,0:T(8,128)S(1)}, f32[64,128]{1,0:T(8,128)S(1)}, u32[]{:S(2)}, u32[]{:S(2)}) collective-permute-start(f32[64,128]{1,0:T(8,128)S(1)} %add_add_fusion.3), channel_id=1, source_target_pairs={{0,8},{8,0},{16,24},{24,16},{1,9},{9,1},{17,25},{25,17},{2,10},{10... | collective-permute-start | bytes 98312 | tf_op jit(solution)/shard_map/ppermute | solution.py:49
  35.1 4.1 %collective-permute-start.14 = (f32[64,128]{1,0:T(8,128)S(1)}, f32[64,128]{1,0:T(8,128)S(1)}, u32[]{:S(2)}, u32[]{:S(2)}) collective-permute-start(f32[64,128]{1,0:T(8,128)S(1)} %add_add_fusion.3), channel_id=1, source_target_pairs={{0,16},{8,24},{16,0},{24,8},{1,17},{9,25},{17,1},{25,9},{2,18},{10... | collective-permute-start | bytes 98312 | tf_op jit(solution)/shard_map/ppermute | solution.py:49
  41.4 5.8 %collective-permute-start.18 = (f32[64,384]{1,0:T(8,128)S(1)}, f32[64,384]{1,0:T(8,128)S(1)}, u32[]{:S(2)}, u32[]{:S(2)}) collective-permute-start(f32[64,384]{1,0:T(8,128)S(1)} %get-tuple-element.136.refs_0_), channel_id=1, source_target_pairs={{0,24},{8,16},{16,8},{24,0},{1,25},{9,17},{17,9},{25,1},{2,26},{10... | collective-permute-start | bytes 294920 | tf_op jit(solution)/shard_map/ppermute | solution.py:36
  43.0 5.8 %collective-permute-start.19 = (f32[64,384]{1,0:T(8,128)S(1)}, f32[64,384]{1,0:T(8,128)S(1)}, u32[]{:S(2)}, u32[]{:S(2)}) collective-permute-start(f32[64,384]{1,0:T(8,128)S(1)} %get-tuple-element.137.refs_1_), channel_id=1, source_target_pairs={{0,7},{1,2},{2,1},{3,4},{4,3},{5,6},{6,5},{7,0},{8,15},{9,10},{10,... | collective-permute-start | bytes 294920 | tf_op jit(solution)/shard_map/ppermute | solution.py:36
  44.3 5.0 %collective-permute-start.20 = (f32[64,384]{1,0:T(8,128)S(1)}, f32[64,384]{1,0:T(8,128)S(1)}, u32[]{:S(2)}, u32[]{:S(2)}) collective-permute-start(f32[64,384]{1,0:T(8,128)S(1)} %get-tuple-element.138.refs_2_), channel_id=1, source_target_pairs={{0,8},{8,0},{16,24},{24,16},{1,9},{9,1},{17,25},{25,17},{2,10},{10... | collective-permute-start | bytes 294920 | tf_op jit(solution)/shard_map/ppermute | solution.py:36
  44.9 4.5 %collective-permute-start.21 = (f32[64,384]{1,0:T(8,128)S(1)}, f32[64,384]{1,0:T(8,128)S(1)}, u32[]{:S(2)}, u32[]{:S(2)}) collective-permute-start(f32[64,384]{1,0:T(8,128)S(1)} %get-tuple-element.139.refs_3_), channel_id=1, source_target_pairs={{0,1},{1,0},{2,3},{3,2},{4,5},{5,4},{6,7},{7,6},{8,9},{9,8},{10,11... | collective-permute-start | bytes 294920 | tf_op jit(solution)/shard_map/ppermute | solution.py:36
  50.5 1.5 %collective-permute-start.23 = (f32[64,512]{1,0:T(8,128)S(1)}, f32[64,512]{1,0:T(8,128)S(1)}, u32[]{:S(2)}, u32[]{:S(2)}) collective-permute-start(f32[64,512]{1,0:T(8,128)S(1)} %get-tuple-element.148.own_core), channel_id=1, source_target_pairs={{0,1},{1,0},{2,3},{3,2},{4,5},{5,4},{6,7},{7,6},{8,9},{9,8},{10,11... | collective-permute-start | bytes 393224 | tf_op jit(solution)/shard_map/ppermute | solution.py:36
  50.6 6.5 %collective-permute-start.22 = (f32[64,384]{1,0:T(8,128)S(1)}, f32[64,384]{1,0:T(8,128)S(1)}, u32[]{:S(2)}, u32[]{:S(2)}) collective-permute-start(f32[64,384]{1,0:T(8,128)S(1)} %get-tuple-element.146.own_far), channel_id=1, source_target_pairs={{0,24},{8,16},{16,8},{24,0},{1,25},{9,17},{17,9},{25,1},{2,26},{10... | collective-permute-start | bytes 294920 | tf_op jit(solution)/shard_map/ppermute | solution.py:36
  52.0 5.9 %collective-permute-start.26 = (f32[64,128]{1,0:T(8,128)S(1)}, f32[64,128]{1,0:T(8,128)S(1)}, u32[]{:S(2)}, u32[]{:S(2)}) collective-permute-start(f32[64,128]{1,0:T(8,128)S(1)} %slice_add_fusion), channel_id=1, source_target_pairs={{0,6},{1,7},{2,4},{3,5},{4,2},{5,3},{6,0},{7,1},{8,14},{9,15},{10,... | collective-permute-start | bytes 98312 | tf_op jit(solution)/shard_map/ppermute | solution.py:49
  53.9 4.3 %collective-permute-start.25 = (f32[64,128]{1,0:T(8,128)S(1)}, f32[64,128]{1,0:T(8,128)S(1)}, u32[]{:S(2)}, u32[]{:S(2)}) collective-permute-start(f32[64,128]{1,0:T(8,128)S(1)} %slice_add_fusion), channel_id=1, source_target_pairs={{0,2},{1,3},{2,0},{3,1},{4,6},{5,7},{6,4},{7,5},{8,10},{9,11},{10,... | collective-permute-start | bytes 98312 | tf_op jit(solution)/shard_map/ppermute | solution.py:49
  53.9 5.1 %collective-permute-start.24 = (f32[64,128]{1,0:T(8,128)S(1)}, f32[64,128]{1,0:T(8,128)S(1)}, u32[]{:S(2)}, u32[]{:S(2)}) collective-permute-start(f32[64,128]{1,0:T(8,128)S(1)} %slice_add_fusion), channel_id=1, source_target_pairs={{0,4},{1,5},{2,6},{3,7},{4,0},{5,1},{6,2},{7,3},{8,12},{9,13},{10,... | collective-permute-start | bytes 98312 | tf_op jit(solution)/shard_map/ppermute | solution.py:49
  56.4 6.5 %collective-permute-start.31 = (f32[64,384]{1,0:T(8,128)S(1)}, f32[64,384]{1,0:T(8,128)S(1)}, u32[]{:S(2)}, u32[]{:S(2)}) collective-permute-start(f32[64,384]{1,0:T(8,128)S(1)} %get-tuple-element.164.own_near), channel_id=1, source_target_pairs={{0,8},{8,0},{16,24},{24,16},{1,9},{9,1},{17,25},{25,17},{2,10},{10... | collective-permute-start | bytes 294920 | tf_op jit(solution)/shard_map/ppermute | solution.py:36
  59.0 6.8 %collective-permute-start.27 = (f32[64,384]{1,0:T(8,128)S(1)}, f32[64,384]{1,0:T(8,128)S(1)}, u32[]{:S(2)}, u32[]{:S(2)}) collective-permute-start(f32[64,384]{1,0:T(8,128)S(1)} %get-tuple-element.156.own_high), channel_id=1, source_target_pairs={{0,7},{1,2},{2,1},{3,4},{4,3},{5,6},{6,5},{7,0},{8,15},{9,10},{10,... | collective-permute-start | bytes 294920 | tf_op jit(solution)/shard_map/ppermute | solution.py:36
  59.5 4.8 %collective-permute-start.30 = (f32[64,128]{1,0:T(8,128)S(1)}, f32[64,128]{1,0:T(8,128)S(1)}, u32[]{:S(2)}, u32[]{:S(2)}) collective-permute-start(f32[64,128]{1,0:T(8,128)S(1)} %add_add_fusion.1), channel_id=1, source_target_pairs={{0,24},{8,16},{16,8},{24,0},{1,25},{9,17},{17,9},{25,1},{2,26},{10... | collective-permute-start | bytes 98312 | tf_op jit(solution)/shard_map/ppermute | solution.py:49
  61.1 4.1 %collective-permute-start.29 = (f32[64,128]{1,0:T(8,128)S(1)}, f32[64,128]{1,0:T(8,128)S(1)}, u32[]{:S(2)}, u32[]{:S(2)}) collective-permute-start(f32[64,128]{1,0:T(8,128)S(1)} %add_add_fusion.1), channel_id=1, source_target_pairs={{0,8},{8,0},{16,24},{24,16},{1,9},{9,1},{17,25},{25,17},{2,10},{10... | collective-permute-start | bytes 98312 | tf_op jit(solution)/shard_map/ppermute | solution.py:49
  61.6 4.2 %collective-permute-start.28 = (f32[64,128]{1,0:T(8,128)S(1)}, f32[64,128]{1,0:T(8,128)S(1)}, u32[]{:S(2)}, u32[]{:S(2)}) collective-permute-start(f32[64,128]{1,0:T(8,128)S(1)} %add_add_fusion.1), channel_id=1, source_target_pairs={{0,16},{8,24},{16,0},{24,8},{1,17},{9,25},{17,1},{25,9},{2,18},{10... | collective-permute-start | bytes 98312 | tf_op jit(solution)/shard_map/ppermute | solution.py:49
  (5 other events, 37.5 us)
where the time goes:
time: 67.6 us; the launch traced here: 67.4 us
  starting transfers between devices  35.9 us (53%)
  Pallas kernels  15.5 us (23%)
  waiting for transfers between devices  14 us (21%)
  other arithmetic  1.13 us (2%)
  between operations  0.89 us (1%)
    ppermute x20, starting transfers between devices, swap(): return lax.ppermute(face, axis, pairs)  20 us
    ppermute x12, starting transfers between devices, sum_over(): lax.ppermute(values, axis, [(i, i ^ k * step) for i in range(peers)])  15.9 us
    pallas_call x11, Pallas kernels, call(): pl.pallas_call(kernel, in_specs=specs, out_specs=[VMEM] * len(outs), out_...  15.5 us
    ppermute x12, waiting for transfers between devices, sum_over(): lax.ppermute(values, axis, [(i, i ^ k * step) for i in range(peers)])  8.12 us
    ppermute x20, waiting for transfers between devices, swap(): return lax.ppermute(face, axis, pairs)  5.87 us
  transfers between devices with their start and end apart: 32, of which 16 were waited for; matrix products, arithmetic and copies ran while one was open for 0% of the time, Pallas kernels for 12%

commit v1 on v0

--- a/solution.py
+++ b/solution.py
@@ -37,7 +37,12 @@
 
 
 def exchange(faces):
-    return lax.optimization_barrier([swap(face, i) for i, face in enumerate(faces)])
+    order = (0, 2, 1, 3)
+    far, near, high, core = [
+        swap(face, i)
+        for i, face in zip(order, lax.optimization_barrier([faces[i] for i in order]))
+    ]
+    return [far, high, near, core]
 
 
 def sum_over(values, axis, step, before=(), after=()):

time: 67.6 us -> 69.4 us (1.027)
  waiting for transfers between devices: 14 us -> 15.3 us
    ppermute x20, waiting for transfers between devices: 5.87 us -> 7.38 us  [swap(): return lax.ppermute(face, axis, pairs)]
  transfers between devices with their start and end apart: 32 -> 32, of which waited for: 16 -> 17; matrix products, arithmetic and copies ran while one was open for 0% -> 0% of each run, Pallas kernels for 12% -> 11%
where the time goes in v1:
time: 69.4 us; the launch traced here: 69.2 us
  starting transfers between devices  36.4 us (52%)
  Pallas kernels  15.5 us (22%)
  waiting for transfers between devices  15.3 us (22%)
  other arithmetic  1.13 us (2%)
  between operations  0.88 us (1%)
    ppermute x20, starting transfers between devices, swap(): return lax.ppermute(face, axis, pairs)  20.5 us
    ppermute x12, starting transfers between devices, sum_over(): lax.ppermute(values, axis, [(i, i ^ k * step) for i in range(peers)])  15.9 us
    pallas_call x11, Pallas kernels, call(): pl.pallas_call(kernel, in_specs=specs, out_specs=[VMEM] * len(outs), out_...  15.5 us
    ppermute x12, waiting for transfers between devices, sum_over(): lax.ppermute(values, axis, [(i, i ^ k * step) for i in range(peers)])  7.96 us
    ppermute x20, waiting for transfers between devices, swap(): return lax.ppermute(face, axis, pairs)  7.38 us
  transfers between devices with their start and end apart: 32, of which 17 were waited for; matrix products, arithmetic and copies ran while one was open for 0% of the time, Pallas kernels for 11%

profile of v1, /device:TPU:0, one launch (start us, length us, event | category | flops | bytes accessed | tf_op | source)
XLA Modules:
  0.0 69.2 jit_solution(10421961557831655937)
XLA Ops:
  0.6 1.1 %slice_select_fusion = (f32[64,384]{1,0:T(8,128)S(1)}, f32[64,384]{1,0:T(8,128)S(1)}, f32[64,384]{1,0:T(8,128)S(1)}, f32[64,384]{1,0:T(8,128)S(1)}) fusion(f32[64,1536]{1,0:T(8,128)} %bitcast.16, pred[]{:T(512)S(6)} %eq.10, pred[]{:T(512)S(6)} %eq.9), kind=kLoop, calls=%fused_computation.1 | loop fusion | flops 98304 | bytes 786434 | tf_op jit(solution)/shard_map/jit(_where)/select_n | solution.py:25
  1.7 4.0 %collective-permute-start = (f32[64,384]{1,0:T(8,128)S(1)}, f32[64,384]{1,0:T(8,128)S(1)}, u32[]{:S(2)}, u32[]{:S(2)}) collective-permute-start(f32[64,384]{1,0:T(8,128)S(1)} %get-tuple-element.92), channel_id=1, source_target_pairs={{0,24},{8,16},{16,8},{24,0},{1,25},{9,17},{17,9},{25,1},{2,26},{10... | collective-permute-start | bytes 294920 | tf_op jit(solution)/shard_map/ppermute | solution.py:36
  5.7 2.8 %collective-permute-start.1 = (f32[64,384]{1,0:T(8,128)S(1)}, f32[64,384]{1,0:T(8,128)S(1)}, u32[]{:S(2)}, u32[]{:S(2)}) collective-permute-start(f32[64,384]{1,0:T(8,128)S(1)} %get-tuple-element.93), channel_id=1, source_target_pairs={{0,7},{1,2},{2,1},{3,4},{4,3},{5,6},{6,5},{7,0},{8,15},{9,10},{10,... | collective-permute-start | bytes 294920 | tf_op jit(solution)/shard_map/ppermute | solution.py:36
  9.0 2.7 %shard_map.86 = (f32[64,1536]{1,0:T(8,128)S(1)}, bf16[1536,384]{1,0:T(8,128)(2,1)S(1)}, bf16[1536,1536]{1,0:T(8,128)(2,1)S(1)}) custom-call(f32[64,1536]{1,0:T(8,128)} %bitcast.17, s32[4,384]{1,0:T(4,128)} %bitcast.18, bf16[1536,1536]{1,0:T(8,128)(2,1)} %bitcast.15), custom_call_target="tpu_custom_call" | custom-call | flops 301989888 | bytes 4194304 | tf_op jit(solution)/shard_map/pallas_call | solution.py:505
  13.1 1.5 %shard_map.87 = (f32[64,1536]{1,0:T(8,128)S(1)}, f32[64,384]{1,0:T(8,128)S(1)}, f32[64,384]{1,0:T(8,128)S(1)}, f32[64,384]{1,0:T(8,128)S(1)}, f32[64,384]{1,0:T(8,128)S(1)}) custom-call(f32[64,384]{1,0:T(8,128)S(1)} %collective-permute-done.near0, f32[64,384]{1,0:T(8,128)S(1)} %collective-permute-done.1.near1, f32[64,384]{1,0:T(8,128)S(1)} %collective-permute-done.2.near2, ...), custom_call_target="tpu_custom_call" | custom-call | flops 301989888 | bytes 4194304 | tf_op jit(solution)/shard_map/pallas_call | solution.py:505
  15.1 1.5 %collective-permute-start.5 = (f32[64,384]{1,0:T(8,128)S(1)}, f32[64,384]{1,0:T(8,128)S(1)}, u32[]{:S(2)}, u32[]{:S(2)}) collective-permute-start(f32[64,384]{1,0:T(8,128)S(1)} %get-tuple-element.104.refs_2_), channel_id=1, source_target_pairs={{0,8},{8,0},{16,24},{24,16},{1,9},{9,1},{17,25},{25,17},{2,10},{10... | collective-permute-start | bytes 294920 | tf_op jit(solution)/shard_map/ppermute | solution.py:36
  17.9 3.1 %shard_map.89.refs_11_ = bf16[1536,1536]{1,0:T(8,128)(2,1)S(1)} custom-call(bf16[1536,1536]{1,0:T(8,128)(2,1)S(1)} %bitcast.12, bf16[1536,384]{1,0:T(8,128)(2,1)S(1)} %get-tuple-element.97.hots_ref), custom_call_target="tpu_custom_call" | custom-call | flops 603979776 | bytes 4194304 | tf_op jit(solution)/shard_map/pallas_call | solution.py:505
  21.1 1.4 %collective-permute-done.6.refs_6_ = f32[64,384]{1,0:T(8,128)S(1)} collective-permute-done((f32[64,384]{1,0:T(8,128)S(1)}, f32[64,384]{1,0:T(8,128)S(1)}, u32[]{:S(2)}, u32[]{:S(2)}) %collective-permute-start.6) | collective-permute-done | bytes 98336 | tf_op jit(solution)/shard_map/ppermute | solution.py:36
  22.5 1.2 %shard_map.90 = (f32[64,1536]{1,0:T(8,128)S(1)}, f32[80,384]{1,0:T(8,128)S(1)}, f32[80,384]{1,0:T(8,128)S(1)}, f32[80,384]{1,0:T(8,128)S(1)}, f32[80,512]{1,0:T(8,128)S(1)}) custom-call(f32[64,384]{1,0:T(8,128)S(1)} %get-tuple-element.103.refs_0_, f32[64,384]{1,0:T(8,128)S(1)} %get-tuple-element.105.refs_1_, f32[64,384]{1,0:T(8,128)S(1)} %get-tuple-element.104.refs_2_, ...), custom_call_target="tpu_custom_call" | custom-call | flops 301989888 | bytes 4194304 | tf_op jit(solution)/shard_map/pallas_call | solution.py:505
  23.8 1.7 %collective-permute-start.8 = (f32[80,384]{1,0:T(8,128)S(1)}, f32[80,384]{1,0:T(8,128)S(1)}, u32[]{:S(2)}, u32[]{:S(2)}) collective-permute-start(f32[80,384]{1,0:T(8,128)S(1)} %get-tuple-element.114.own0.refs_13_), channel_id=1, source_target_pairs={{0,24},{8,16},{16,8},{24,0},{1,25},{9,17},{17,9},{25,1},{2,26},{10... | collective-permute-start | bytes 368648 | tf_op jit(solution)/shard_map/ppermute | solution.py:36
  25.5 1.8 %collective-permute-start.12 = (f32[64,128]{1,0:T(8,128)S(1)}, f32[64,128]{1,0:T(8,128)S(1)}, u32[]{:S(2)}, u32[]{:S(2)}) collective-permute-start(f32[64,128]{1,0:T(8,128)S(1)} %slice_add_fusion.1), channel_id=1, source_target_pairs={{0,6},{1,7},{2,4},{3,5},{4,2},{5,3},{6,0},{7,1},{8,14},{9,15},{10,... | collective-permute-start | bytes 98312 | tf_op jit(solution)/shard_map/ppermute | solution.py:54
  27.3 2.6 %collective-permute-start.10 = (f32[64,128]{1,0:T(8,128)S(1)}, f32[64,128]{1,0:T(8,128)S(1)}, u32[]{:S(2)}, u32[]{:S(2)}) collective-permute-start(f32[64,128]{1,0:T(8,128)S(1)} %slice_add_fusion.1), channel_id=1, source_target_pairs={{0,4},{1,5},{2,6},{3,7},{4,0},{5,1},{6,2},{7,3},{8,12},{9,13},{10,... | collective-permute-start | bytes 98312 | tf_op jit(solution)/shard_map/ppermute | solution.py:54
  29.9 1.4 %collective-permute-start.17 = (f32[80,384]{1,0:T(8,128)S(1)}, f32[80,384]{1,0:T(8,128)S(1)}, u32[]{:S(2)}, u32[]{:S(2)}) collective-permute-start(f32[80,384]{1,0:T(8,128)S(1)} %get-tuple-element.132.own2.refs_15_), channel_id=1, source_target_pairs={{0,8},{8,0},{16,24},{24,16},{1,9},{9,1},{17,25},{25,17},{2,10},{10... | collective-permute-start | bytes 368648 | tf_op jit(solution)/shard_map/ppermute | solution.py:36
  32.9 1.4 %collective-permute-start.16 = (f32[64,128]{1,0:T(8,128)S(1)}, f32[64,128]{1,0:T(8,128)S(1)}, u32[]{:S(2)}, u32[]{:S(2)}) collective-permute-start(f32[64,128]{1,0:T(8,128)S(1)} %add_add_fusion.3), channel_id=1, source_target_pairs={{0,24},{8,16},{16,8},{24,0},{1,25},{9,17},{17,9},{25,1},{2,26},{10... | collective-permute-start | bytes 98312 | tf_op jit(solution)/shard_map/ppermute | solution.py:54
  34.3 1.3 %collective-permute-start.15 = (f32[64,128]{1,0:T(8,128)S(1)}, f32[64,128]{1,0:T(8,128)S(1)}, u32[]{:S(2)}, u32[]{:S(2)}) collective-permute-start(f32[64,128]{1,0:T(8,128)S(1)} %add_add_fusion.3), channel_id=1, source_target_pairs={{0,8},{8,0},{16,24},{24,16},{1,9},{9,1},{17,25},{25,17},{2,10},{10... | collective-permute-start | bytes 98312 | tf_op jit(solution)/shard_map/ppermute | solution.py:54
  36.7 1.0 %collective-permute-done.16 = f32[64,128]{1,0:T(8,128)S(1)} collective-permute-done((f32[64,128]{1,0:T(8,128)S(1)}, f32[64,128]{1,0:T(8,128)S(1)}, u32[]{:S(2)}, u32[]{:S(2)}) %collective-permute-start.16) | collective-permute-done | bytes 32800 | tf_op jit(solution)/shard_map/ppermute | solution.py:54
  38.6 1.3 %collective-permute-done.14 = f32[64,128]{1,0:T(8,128)S(1)} collective-permute-done((f32[64,128]{1,0:T(8,128)S(1)}, f32[64,128]{1,0:T(8,128)S(1)}, u32[]{:S(2)}, u32[]{:S(2)}) %collective-permute-start.14) | collective-permute-done | bytes 32800 | tf_op jit(solution)/shard_map/ppermute | solution.py:54
  40.1 1.9 %shard_map.93 = (f32[64,1536]{1,0:T(8,128)S(1)}, f32[64,1536]{1,0:T(8,128)S(1)}, f32[64,128]{1,0:T(8,128)S(1)}, f32[64,384]{1,0:T(8,128)S(1)}, f32[64,384]{1,0:T...) custom-call(f32[64,128]{1,0:T(8,128)S(1)} %add_add_fusion.2.sums_ref.first_ref, ...), custom_call_target="tpu_custom_call" | custom-call | flops 301989888 | bytes 4194304 | tf_op jit(solution)/shard_map/pallas_call | solution.py:505
  42.0 1.7 %collective-permute-start.18 = (f32[64,384]{1,0:T(8,128)S(1)}, f32[64,384]{1,0:T(8,128)S(1)}, u32[]{:S(2)}, u32[]{:S(2)}) collective-permute-start(f32[64,384]{1,0:T(8,128)S(1)} %get-tuple-element.140.refs_0_), channel_id=1, source_target_pairs={{0,24},{8,16},{16,8},{24,0},{1,25},{9,17},{17,9},{25,1},{2,26},{10... | collective-permute-start | bytes 294920 | tf_op jit(solution)/shard_map/ppermute | solution.py:36
  45.5 3.1 %collective-permute-done.18.refs_4_ = f32[64,384]{1,0:T(8,128)S(1)} collective-permute-done((f32[64,384]{1,0:T(8,128)S(1)}, f32[64,384]{1,0:T(8,128)S(1)}, u32[]{:S(2)}, u32[]{:S(2)}) %collective-permute-start.18) | collective-permute-done | bytes 98336 | tf_op jit(solution)/shard_map/ppermute | solution.py:36
  49.0 1.1 %collective-permute-done.20.refs_6_ = f32[64,384]{1,0:T(8,128)S(1)} collective-permute-done((f32[64,384]{1,0:T(8,128)S(1)}, f32[64,384]{1,0:T(8,128)S(1)}, u32[]{:S(2)}, u32[]{:S(2)}) %collective-permute-start.20) | collective-permute-done | bytes 98336 | tf_op jit(solution)/shard_map/ppermute | solution.py:36
  50.1 1.2 %shard_map.94 = (f32[64,1536]{1,0:T(8,128)S(1)}, f32[64,384]{1,0:T(8,128)S(1)}, f32[64,384]{1,0:T(8,128)S(1)}, f32[64,384]{1,0:T(8,128)S(1)}, f32[64,512]{1,0:T(8,128)S(1)}) custom-call(f32[64,384]{1,0:T(8,128)S(1)} %get-tuple-element.140.refs_0_, f32[64,384]{1,0:T(8,128)S(1)} %get-tuple-element.142.refs_1_, f32[64,384]{1,0:T(8,128)S(1)} %get-tuple-element.141.refs_2_, ...), custom_call_target="tpu_custom_call" | custom-call | flops 301989888 | bytes 4194304 | tf_op jit(solution)/shard_map/pallas_call | solution.py:505
  51.3 1.6 %collective-permute-start.22 = (f32[64,384]{1,0:T(8,128)S(1)}, f32[64,384]{1,0:T(8,128)S(1)}, u32[]{:S(2)}, u32[]{:S(2)}) collective-permute-start(f32[64,384]{1,0:T(8,128)S(1)} %get-tuple-element.146.own_far), channel_id=1, source_target_pairs={{0,24},{8,16},{16,8},{24,0},{1,25},{9,17},{17,9},{25,1},{2,26},{10... | collective-permute-start | bytes 294920 | tf_op jit(solution)/shard_map/ppermute | solution.py:36
  52.9 2.0 %collective-permute-start.26 = (f32[64,128]{1,0:T(8,128)S(1)}, f32[64,128]{1,0:T(8,128)S(1)}, u32[]{:S(2)}, u32[]{:S(2)}) collective-permute-start(f32[64,128]{1,0:T(8,128)S(1)} %slice_add_fusion), channel_id=1, source_target_pairs={{0,6},{1,7},{2,4},{3,5},{4,2},{5,3},{6,0},{7,1},{8,14},{9,15},{10,... | collective-permute-start | bytes 98312 | tf_op jit(solution)/shard_map/ppermute | solution.py:54
  54.8 2.5 %collective-permute-start.24 = (f32[64,128]{1,0:T(8,128)S(1)}, f32[64,128]{1,0:T(8,128)S(1)}, u32[]{:S(2)}, u32[]{:S(2)}) collective-permute-start(f32[64,128]{1,0:T(8,128)S(1)} %slice_add_fusion), channel_id=1, source_target_pairs={{0,4},{1,5},{2,6},{3,7},{4,0},{5,1},{6,2},{7,3},{8,12},{9,13},{10,... | collective-permute-start | bytes 98312 | tf_op jit(solution)/shard_map/ppermute | solution.py:54
  57.3 1.3 %collective-permute-start.31 = (f32[64,384]{1,0:T(8,128)S(1)}, f32[64,384]{1,0:T(8,128)S(1)}, u32[]{:S(2)}, u32[]{:S(2)}) collective-permute-start(f32[64,384]{1,0:T(8,128)S(1)} %get-tuple-element.164.own_near), channel_id=1, source_target_pairs={{0,8},{8,0},{16,24},{24,16},{1,9},{9,1},{17,25},{25,17},{2,10},{10... | collective-permute-start | bytes 294920 | tf_op jit(solution)/shard_map/ppermute | solution.py:36
  60.4 1.4 %collective-permute-start.30 = (f32[64,128]{1,0:T(8,128)S(1)}, f32[64,128]{1,0:T(8,128)S(1)}, u32[]{:S(2)}, u32[]{:S(2)}) collective-permute-start(f32[64,128]{1,0:T(8,128)S(1)} %add_add_fusion.1), channel_id=1, source_target_pairs={{0,24},{8,16},{16,8},{24,0},{1,25},{9,17},{17,9},{25,1},{2,26},{10... | collective-permute-start | bytes 98312 | tf_op jit(solution)/shard_map/ppermute | solution.py:54
  61.8 1.5 %collective-permute-start.29 = (f32[64,128]{1,0:T(8,128)S(1)}, f32[64,128]{1,0:T(8,128)S(1)}, u32[]{:S(2)}, u32[]{:S(2)}) collective-permute-start(f32[64,128]{1,0:T(8,128)S(1)} %add_add_fusion.1), channel_id=1, source_target_pairs={{0,8},{8,0},{16,24},{24,16},{1,9},{9,1},{17,25},{25,17},{2,10},{10... | collective-permute-start | bytes 98312 | tf_op jit(solution)/shard_map/ppermute | solution.py:54
  63.9 1.3 %shard_map.95 = (f32[64,1536]{1,0:T(8,128)S(1)}, f32[64,1536]{1,0:T(8,128)S(1)}, f32[64,1536]{1,0:T(8,128)S(1)}, f32[64,1536]{1,0:T(8,128)S(1)}, bf16[256,1536]{1,0:T(8,128)(2,1)S(1)}, /*index=5*/f32[64,768]{1,0:T(8,128)S(1)}) custom-call(f32[64,1536]{1,0:T(8,128)S(1)} %get-tuple-element.144.refs_10_.residual_ref, ...), custom_call_target="tpu_custom_call" | custom-call | flops 150994944 | bytes 4194304 | tf_op jit(solution)/shard_map/pallas_call | solution.py:505
  65.2 0.9 %collective-permute-done.29 = f32[64,128]{1,0:T(8,128)S(1)} collective-permute-done((f32[64,128]{1,0:T(8,128)S(1)}, f32[64,128]{1,0:T(8,128)S(1)}, u32[]{:S(2)}, u32[]{:S(2)}) %collective-permute-start.29) | collective-permute-done | bytes 32800 | tf_op jit(solution)/shard_map/ppermute | solution.py:54
  66.1 1.5 %collective-permute-done.28 = f32[64,128]{1,0:T(8,128)S(1)} collective-permute-done((f32[64,128]{1,0:T(8,128)S(1)}, f32[64,128]{1,0:T(8,128)S(1)}, u32[]{:S(2)}, u32[]{:S(2)}) %collective-permute-start.28) | collective-permute-done | bytes 32800 | tf_op jit(solution)/shard_map/ppermute | solution.py:54
  67.6 1.6 %shard_map.96 = (f32[64,4,384]{2,1,0:T(4,128)}, f32[64,4,384]{2,1,0:T(4,128)}) custom-call(f32[64,128]{1,0:T(8,128)S(1)} %add_add_fusion.2.sums_ref.first_ref, f32[64,128]{1,0:T(8,128)S(1)} %add_add_fusion.sums_ref, bf16[384,128]{1,0:T(8,128)(2,1)S(1)} %get-tuple-element.128.down_ref, bf16[128,384]{1,0:T(8,128)(2,1)S(1)} %get-tuple-element.129.up_ref, ...), custom_call_target="tpu_custom_call" | custom-call | flops 75497472 | bytes 4194304 | tf_op jit(solution)/shard_map/pallas_call | solution.py:505
  (63 shorter events, 12.1 us)
Async XLA Ops:
  1.7 9.9 %collective-permute-start = (f32[64,384]{1,0:T(8,128)S(1)}, f32[64,384]{1,0:T(8,128)S(1)}, u32[]{:S(2)}, u32[]{:S(2)}) collective-permute-start(f32[64,384]{1,0:T(8,128)S(1)} %get-tuple-element.92), channel_id=1, source_target_pairs={{0,24},{8,16},{16,8},{24,0},{1,25},{9,17},{17,9},{25,1},{2,26},{10... | collective-permute-start | bytes 294920 | tf_op jit(solution)/shard_map/ppermute | solution.py:36
  5.7 6.6 %collective-permute-start.1 = (f32[64,384]{1,0:T(8,128)S(1)}, f32[64,384]{1,0:T(8,128)S(1)}, u32[]{:S(2)}, u32[]{:S(2)}) collective-permute-start(f32[64,384]{1,0:T(8,128)S(1)} %get-tuple-element.93), channel_id=1, source_target_pairs={{0,7},{1,2},{2,1},{3,4},{4,3},{5,6},{6,5},{7,0},{8,15},{9,10},{10,... | collective-permute-start | bytes 294920 | tf_op jit(solution)/shard_map/ppermute | solution.py:36
  8.4 4.6 %collective-permute-start.2 = (f32[64,384]{1,0:T(8,128)S(1)}, f32[64,384]{1,0:T(8,128)S(1)}, u32[]{:S(2)}, u32[]{:S(2)}) collective-permute-start(f32[64,384]{1,0:T(8,128)S(1)} %get-tuple-element.94), channel_id=1, source_target_pairs={{0,8},{8,0},{16,24},{24,16},{1,9},{9,1},{17,25},{25,17},{2,10},{10... | collective-permute-start | bytes 294920 | tf_op jit(solution)/shard_map/ppermute | solution.py:36
  9.0 4.1 %collective-permute-start.3 = (f32[64,384]{1,0:T(8,128)S(1)}, f32[64,384]{1,0:T(8,128)S(1)}, u32[]{:S(2)}, u32[]{:S(2)}) collective-permute-start(f32[64,384]{1,0:T(8,128)S(1)} %get-tuple-element.95), channel_id=1, source_target_pairs={{0,1},{1,0},{2,3},{3,2},{4,5},{5,4},{6,7},{7,6},{8,9},{9,8},{10,11... | collective-permute-start | bytes 294920 | tf_op jit(solution)/shard_map/ppermute | solution.py:36
  14.6 6.5 %collective-permute-start.4 = (f32[64,384]{1,0:T(8,128)S(1)}, f32[64,384]{1,0:T(8,128)S(1)}, u32[]{:S(2)}, u32[]{:S(2)}) collective-permute-start(f32[64,384]{1,0:T(8,128)S(1)} %get-tuple-element.103.refs_0_), channel_id=1, source_target_pairs={{0,24},{8,16},{16,8},{24,0},{1,25},{9,17},{17,9},{25,1},{2,26},{10... | collective-permute-start | bytes 294920 | tf_op jit(solution)/shard_map/ppermute | solution.py:36
  15.1 5.9 %collective-permute-start.5 = (f32[64,384]{1,0:T(8,128)S(1)}, f32[64,384]{1,0:T(8,128)S(1)}, u32[]{:S(2)}, u32[]{:S(2)}) collective-permute-start(f32[64,384]{1,0:T(8,128)S(1)} %get-tuple-element.104.refs_2_), channel_id=1, source_target_pairs={{0,8},{8,0},{16,24},{24,16},{1,9},{9,1},{17,25},{25,17},{2,10},{10... | collective-permute-start | bytes 294920 | tf_op jit(solution)/shard_map/ppermute | solution.py:36
  16.6 5.8 %collective-permute-start.6 = (f32[64,384]{1,0:T(8,128)S(1)}, f32[64,384]{1,0:T(8,128)S(1)}, u32[]{:S(2)}, u32[]{:S(2)}) collective-permute-start(f32[64,384]{1,0:T(8,128)S(1)} %get-tuple-element.105.refs_1_), channel_id=1, source_target_pairs={{0,7},{1,2},{2,1},{3,4},{4,3},{5,6},{6,5},{7,0},{8,15},{9,10},{10,... | collective-permute-start | bytes 294920 | tf_op jit(solution)/shard_map/ppermute | solution.py:36
  17.3 5.2 %collective-permute-start.7 = (f32[64,384]{1,0:T(8,128)S(1)}, f32[64,384]{1,0:T(8,128)S(1)}, u32[]{:S(2)}, u32[]{:S(2)}) collective-permute-start(f32[64,384]{1,0:T(8,128)S(1)} %get-tuple-element.106.refs_3_), channel_id=1, source_target_pairs={{0,1},{1,0},{2,3},{3,2},{4,5},{5,4},{6,7},{7,6},{8,9},{9,8},{10,11... | collective-permute-start | bytes 294920 | tf_op jit(solution)/shard_map/ppermute | solution.py:36
  23.7 1.7 %collective-permute-start.9 = (f32[80,512]{1,0:T(8,128)S(1)}, f32[80,512]{1,0:T(8,128)S(1)}, u32[]{:S(2)}, u32[]{:S(2)}) collective-permute-start(f32[80,512]{1,0:T(8,128)S(1)} %get-tuple-element.116.own3.refs_16_), channel_id=1, source_target_pairs={{0,1},{1,0},{2,3},{3,2},{4,5},{5,4},{6,7},{7,6},{8,9},{9,8},{10,11... | collective-permute-start | bytes 491528 | tf_op jit(solution)/shard_map/ppermute | solution.py:36
  23.8 7.5 %collective-permute-start.8 = (f32[80,384]{1,0:T(8,128)S(1)}, f32[80,384]{1,0:T(8,128)S(1)}, u32[]{:S(2)}, u32[]{:S(2)}) collective-permute-start(f32[80,384]{1,0:T(8,128)S(1)} %get-tuple-element.114.own0.refs_13_), channel_id=1, source_target_pairs={{0,24},{8,16},{16,8},{24,0},{1,25},{9,17},{17,9},{25,1},{2,26},{10... | collective-permute-start | bytes 368648 | tf_op jit(solution)/shard_map/ppermute | solution.py:36
  25.5 5.9 %collective-permute-start.12 = (f32[64,128]{1,0:T(8,128)S(1)}, f32[64,128]{1,0:T(8,128)S(1)}, u32[]{:S(2)}, u32[]{:S(2)}) collective-permute-start(f32[64,128]{1,0:T(8,128)S(1)} %slice_add_fusion.1), channel_id=1, source_target_pairs={{0,6},{1,7},{2,4},{3,5},{4,2},{5,3},{6,0},{7,1},{8,14},{9,15},{10,... | collective-permute-start | bytes 98312 | tf_op jit(solution)/shard_map/ppermute | solution.py:54
  27.3 4.4 %collective-permute-start.11 = (f32[64,128]{1,0:T(8,128)S(1)}, f32[64,128]{1,0:T(8,128)S(1)}, u32[]{:S(2)}, u32[]{:S(2)}) collective-permute-start(f32[64,128]{1,0:T(8,128)S(1)} %slice_add_fusion.1), channel_id=1, source_target_pairs={{0,2},{1,3},{2,0},{3,1},{4,6},{5,7},{6,4},{7,5},{8,10},{9,11},{10,... | collective-permute-start | bytes 98312 | tf_op jit(solution)/shard_map/ppermute | solution.py:54
  27.3 5.2 %collective-permute-start.10 = (f32[64,128]{1,0:T(8,128)S(1)}, f32[64,128]{1,0:T(8,128)S(1)}, u32[]{:S(2)}, u32[]{:S(2)}) collective-permute-start(f32[64,128]{1,0:T(8,128)S(1)} %slice_add_fusion.1), channel_id=1, source_target_pairs={{0,4},{1,5},{2,6},{3,7},{4,0},{5,1},{6,2},{7,3},{8,12},{9,13},{10,... | collective-permute-start | bytes 98312 | tf_op jit(solution)/shard_map/ppermute | solution.py:54
  29.9 6.5 %collective-permute-start.17 = (f32[80,384]{1,0:T(8,128)S(1)}, f32[80,384]{1,0:T(8,128)S(1)}, u32[]{:S(2)}, u32[]{:S(2)}) collective-permute-start(f32[80,384]{1,0:T(8,128)S(1)} %get-tuple-element.132.own2.refs_15_), channel_id=1, source_target_pairs={{0,8},{8,0},{16,24},{24,16},{1,9},{9,1},{17,25},{25,17},{2,10},{10... | collective-permute-start | bytes 368648 | tf_op jit(solution)/shard_map/ppermute | solution.py:36
  32.5 7.4 %collective-permute-start.13 = (f32[80,384]{1,0:T(8,128)S(1)}, f32[80,384]{1,0:T(8,128)S(1)}, u32[]{:S(2)}, u32[]{:S(2)}) collective-permute-start(f32[80,384]{1,0:T(8,128)S(1)} %get-tuple-element.124.own1.refs_14_), channel_id=1, source_target_pairs={{0,7},{1,2},{2,1},{3,4},{4,3},{5,6},{6,5},{7,0},{8,15},{9,10},{10,... | collective-permute-start | bytes 368648 | tf_op jit(solution)/shard_map/ppermute | solution.py:36
  32.9 4.8 %collective-permute-start.16 = (f32[64,128]{1,0:T(8,128)S(1)}, f32[64,128]{1,0:T(8,128)S(1)}, u32[]{:S(2)}, u32[]{:S(2)}) collective-permute-start(f32[64,128]{1,0:T(8,128)S(1)} %add_add_fusion.3), channel_id=1, source_target_pairs={{0,24},{8,16},{16,8},{24,0},{1,25},{9,17},{17,9},{25,1},{2,26},{10... | collective-permute-start | bytes 98312 | tf_op jit(solution)/shard_map/ppermute | solution.py:54
  34.3 4.3 %collective-permute-start.15 = (f32[64,128]{1,0:T(8,128)S(1)}, f32[64,128]{1,0:T(8,128)S(1)}, u32[]{:S(2)}, u32[]{:S(2)}) collective-permute-start(f32[64,128]{1,0:T(8,128)S(1)} %add_add_fusion.3), channel_id=1, source_target_pairs={{0,8},{8,0},{16,24},{24,16},{1,9},{9,1},{17,25},{25,17},{2,10},{10... | collective-permute-start | bytes 98312 | tf_op jit(solution)/shard_map/ppermute | solution.py:54
  35.6 4.2 %collective-permute-start.14 = (f32[64,128]{1,0:T(8,128)S(1)}, f32[64,128]{1,0:T(8,128)S(1)}, u32[]{:S(2)}, u32[]{:S(2)}) collective-permute-start(f32[64,128]{1,0:T(8,128)S(1)} %add_add_fusion.3), channel_id=1, source_target_pairs={{0,16},{8,24},{16,0},{24,8},{1,17},{9,25},{17,1},{25,9},{2,18},{10... | collective-permute-start | bytes 98312 | tf_op jit(solution)/shard_map/ppermute | solution.py:54
  42.0 6.6 %collective-permute-start.18 = (f32[64,384]{1,0:T(8,128)S(1)}, f32[64,384]{1,0:T(8,128)S(1)}, u32[]{:S(2)}, u32[]{:S(2)}) collective-permute-start(f32[64,384]{1,0:T(8,128)S(1)} %get-tuple-element.140.refs_0_), channel_id=1, source_target_pairs={{0,24},{8,16},{16,8},{24,0},{1,25},{9,17},{17,9},{25,1},{2,26},{10... | collective-permute-start | bytes 294920 | tf_op jit(solution)/shard_map/ppermute | solution.py:36
  43.7 5.3 %collective-permute-start.19 = (f32[64,384]{1,0:T(8,128)S(1)}, f32[64,384]{1,0:T(8,128)S(1)}, u32[]{:S(2)}, u32[]{:S(2)}) collective-permute-start(f32[64,384]{1,0:T(8,128)S(1)} %get-tuple-element.141.refs_2_), channel_id=1, source_target_pairs={{0,8},{8,0},{16,24},{24,16},{1,9},{9,1},{17,25},{25,17},{2,10},{10... | collective-permute-start | bytes 294920 | tf_op jit(solution)/shard_map/ppermute | solution.py:36
  44.2 5.8 %collective-permute-start.20 = (f32[64,384]{1,0:T(8,128)S(1)}, f32[64,384]{1,0:T(8,128)S(1)}, u32[]{:S(2)}, u32[]{:S(2)}) collective-permute-start(f32[64,384]{1,0:T(8,128)S(1)} %get-tuple-element.142.refs_1_), channel_id=1, source_target_pairs={{0,7},{1,2},{2,1},{3,4},{4,3},{5,6},{6,5},{7,0},{8,15},{9,10},{10,... | collective-permute-start | bytes 294920 | tf_op jit(solution)/shard_map/ppermute | solution.py:36
  44.9 5.1 %collective-permute-start.21 = (f32[64,384]{1,0:T(8,128)S(1)}, f32[64,384]{1,0:T(8,128)S(1)}, u32[]{:S(2)}, u32[]{:S(2)}) collective-permute-start(f32[64,384]{1,0:T(8,128)S(1)} %get-tuple-element.143.refs_3_), channel_id=1, source_target_pairs={{0,1},{1,0},{2,3},{3,2},{4,5},{5,4},{6,7},{7,6},{8,9},{9,8},{10,11... | collective-permute-start | bytes 294920 | tf_op jit(solution)/shard_map/ppermute | solution.py:36
  51.2 1.6 %collective-permute-start.23 = (f32[64,512]{1,0:T(8,128)S(1)}, f32[64,512]{1,0:T(8,128)S(1)}, u32[]{:S(2)}, u32[]{:S(2)}) collective-permute-start(f32[64,512]{1,0:T(8,128)S(1)} %get-tuple-element.148.own_core), channel_id=1, source_target_pairs={{0,1},{1,0},{2,3},{3,2},{4,5},{5,4},{6,7},{7,6},{8,9},{9,8},{10,11... | collective-permute-start | bytes 393224 | tf_op jit(solution)/shard_map/ppermute | solution.py:36
  51.3 7.4 %collective-permute-start.22 = (f32[64,384]{1,0:T(8,128)S(1)}, f32[64,384]{1,0:T(8,128)S(1)}, u32[]{:S(2)}, u32[]{:S(2)}) collective-permute-start(f32[64,384]{1,0:T(8,128)S(1)} %get-tuple-element.146.own_far), channel_id=1, source_target_pairs={{0,24},{8,16},{16,8},{24,0},{1,25},{9,17},{17,9},{25,1},{2,26},{10... | collective-permute-start | bytes 294920 | tf_op jit(solution)/shard_map/ppermute | solution.py:36
  52.9 5.8 %collective-permute-start.26 = (f32[64,128]{1,0:T(8,128)S(1)}, f32[64,128]{1,0:T(8,128)S(1)}, u32[]{:S(2)}, u32[]{:S(2)}) collective-permute-start(f32[64,128]{1,0:T(8,128)S(1)} %slice_add_fusion), channel_id=1, source_target_pairs={{0,6},{1,7},{2,4},{3,5},{4,2},{5,3},{6,0},{7,1},{8,14},{9,15},{10,... | collective-permute-start | bytes 98312 | tf_op jit(solution)/shard_map/ppermute | solution.py:54
  54.8 4.2 %collective-permute-start.25 = (f32[64,128]{1,0:T(8,128)S(1)}, f32[64,128]{1,0:T(8,128)S(1)}, u32[]{:S(2)}, u32[]{:S(2)}) collective-permute-start(f32[64,128]{1,0:T(8,128)S(1)} %slice_add_fusion), channel_id=1, source_target_pairs={{0,2},{1,3},{2,0},{3,1},{4,6},{5,7},{6,4},{7,5},{8,10},{9,11},{10,... | collective-permute-start | bytes 98312 | tf_op jit(solution)/shard_map/ppermute | solution.py:54
  54.8 5.0 %collective-permute-start.24 = (f32[64,128]{1,0:T(8,128)S(1)}, f32[64,128]{1,0:T(8,128)S(1)}, u32[]{:S(2)}, u32[]{:S(2)}) collective-permute-start(f32[64,128]{1,0:T(8,128)S(1)} %slice_add_fusion), channel_id=1, source_target_pairs={{0,4},{1,5},{2,6},{3,7},{4,0},{5,1},{6,2},{7,3},{8,12},{9,13},{10,... | collective-permute-start | bytes 98312 | tf_op jit(solution)/shard_map/ppermute | solution.py:54
  57.3 6.6 %collective-permute-start.31 = (f32[64,384]{1,0:T(8,128)S(1)}, f32[64,384]{1,0:T(8,128)S(1)}, u32[]{:S(2)}, u32[]{:S(2)}) collective-permute-start(f32[64,384]{1,0:T(8,128)S(1)} %get-tuple-element.164.own_near), channel_id=1, source_target_pairs={{0,8},{8,0},{16,24},{24,16},{1,9},{9,1},{17,25},{25,17},{2,10},{10... | collective-permute-start | bytes 294920 | tf_op jit(solution)/shard_map/ppermute | solution.py:36
  59.9 7.7 %collective-permute-start.27 = (f32[64,384]{1,0:T(8,128)S(1)}, f32[64,384]{1,0:T(8,128)S(1)}, u32[]{:S(2)}, u32[]{:S(2)}) collective-permute-start(f32[64,384]{1,0:T(8,128)S(1)} %get-tuple-element.156.own_high), channel_id=1, source_target_pairs={{0,7},{1,2},{2,1},{3,4},{4,3},{5,6},{6,5},{7,0},{8,15},{9,10},{10,... | collective-permute-start | bytes 294920 | tf_op jit(solution)/shard_map/ppermute | solution.py:36
  60.4 4.8 %collective-permute-start.30 = (f32[64,128]{1,0:T(8,128)S(1)}, f32[64,128]{1,0:T(8,128)S(1)}, u32[]{:S(2)}, u32[]{:S(2)}) collective-permute-start(f32[64,128]{1,0:T(8,128)S(1)} %add_add_fusion.1), channel_id=1, source_target_pairs={{0,24},{8,16},{16,8},{24,0},{1,25},{9,17},{17,9},{25,1},{2,26},{10... | collective-permute-start | bytes 98312 | tf_op jit(solution)/shard_map/ppermute | solution.py:54
  61.8 4.3 %collective-permute-start.29 = (f32[64,128]{1,0:T(8,128)S(1)}, f32[64,128]{1,0:T(8,128)S(1)}, u32[]{:S(2)}, u32[]{:S(2)}) collective-permute-start(f32[64,128]{1,0:T(8,128)S(1)} %add_add_fusion.1), channel_id=1, source_target_pairs={{0,8},{8,0},{16,24},{24,16},{1,9},{9,1},{17,25},{25,17},{2,10},{10... | collective-permute-start | bytes 98312 | tf_op jit(solution)/shard_map/ppermute | solution.py:54
  63.3 4.2 %collective-permute-start.28 = (f32[64,128]{1,0:T(8,128)S(1)}, f32[64,128]{1,0:T(8,128)S(1)}, u32[]{:S(2)}, u32[]{:S(2)}) collective-permute-start(f32[64,128]{1,0:T(8,128)S(1)} %add_add_fusion.1), channel_id=1, source_target_pairs={{0,16},{8,24},{16,0},{24,8},{1,17},{9,25},{17,1},{25,9},{2,18},{10... | collective-permute-start | bytes 98312 | tf_op jit(solution)/shard_map/ppermute | solution.py:54
  (5 other events, 36.1 us)
